TPU v7x, 32 devices: a whole 2x2x4 slice. The times are simulated.
32 devices in a mesh: dp: 8 (over z, x), blk: 4 (over y, core).
Axes of the slice: x: 2, y: 2, z: 4, core: 2. Of those that a mesh axis runs over, the one named last changes fastest.
Arguments:
- inputs: bfloat16 [16, 2048, 768], P('dp', 'blk'), may hold values from -6 to 6
- doc_lengths: int32 [16, 8], P('dp'), may hold values from 0 to 2048, as said below
- norm1_gain: float32 [768], replicated, may hold values from 0.25 to 1.75
- w_query: bfloat16 [768, 768], replicated, may hold values from -0.21875 to 0.21875
- w_key: bfloat16 [768, 768], replicated, may hold values from -0.21875 to 0.21875
- w_value: bfloat16 [768, 768], replicated, may hold values from -0.21875 to 0.21875
- head_mix_pre: float32 [12, 12], replicated, may hold values from -3.5 to 3.5
- head_mix_post: float32 [12, 12], replicated, may hold values from -1.75 to 1.75
- w_attn_out: bfloat16 [768, 768], replicated, may hold values from -1.25 to 1.25
- norm2_gain: float32 [768], replicated, may hold values from 0.25 to 1.75
- w_ff_in: bfloat16 [768, 3072], replicated, may hold values from -0.21875 to 0.21875
- w_ff_out: bfloat16 [3072, 768], replicated, may hold values from -0.109375 to 0.109375
- out_cotangent: bfloat16 [16, 2048, 768], P('dp', 'blk'), may hold values from -6 to 6
Outputs:
- output: bfloat16 [16, 2048, 768], P('dp', 'blk')
- input_grad: bfloat16 [16, 2048, 768], P('dp', 'blk')
- grad_norm1_gain: float32 [768], P(('dp', 'blk'))
- grad_w_query: float32 [768, 768], P(('dp', 'blk'))
- grad_w_key: float32 [768, 768], P(('dp', 'blk'))
- grad_w_value: float32 [768, 768], P(('dp', 'blk'))
- grad_head_mix_pre: float32 [12, 12], replicated
- grad_head_mix_post: float32 [12, 12], replicated
- grad_w_attn_out: float32 [768, 768], P(('dp', 'blk'))
- grad_norm2_gain: float32 [768], P(('dp', 'blk'))
- grad_w_ff_in: float32 [768, 3072], P(('dp', 'blk'))
- grad_w_ff_out: float32 [3072, 768], P(('dp', 'blk'))
Inputs may be any that keep to these rules, and one draw needn't show every extreme that they name: `doc_lengths`: each row lists its documents' lengths in order, multiples of 256 that sum to 2048, with zeros after the last document. Among the rows of one index of dp, one is a single document of 2048 tokens.
All inputs are finite; a program needn't handle non-finite values.
Results may differ from a plain program's by a relative error of at most 0.015.
The roundings to bfloat16 on the way count: a program that leaves them out, or rounds other values in their place, can miss the bound.
Values may be sent and summed in bfloat16 or wider, within the bound.
No kernel may reach another device: no remote copies, remote signals or barrier semaphores. Data moves between devices by JAX's collectives and lax.ppermute only.
A program may use at most 384 MiB of HBM per device.

v0:
```python
import jax
import jax.numpy as jnp
from jax import lax
from jax.sharding import PartitionSpec as P

HEAD_DIM = 64


EPSILON = 1e-06
MASKED = -1e30
PRECISE = lax.Precision.HIGHEST


def from_behind(block, axis, distance):
    devices = range(lax.axis_size(axis))
    route = [(i - distance, i) for i in devices if i - distance in devices]
    return lax.ppermute(block, axis, route)


def from_behind_2(x, axis, by):
    size = lax.axis_size(axis)
    return lax.ppermute(x, axis, [(i, (i + by) % size) for i in range(size)])


def rms_norm(values, scales):
    factor = lax.rsqrt(jnp.mean(values * values, axis=-1, keepdims=True) + EPSILON)
    return values * factor * scales


def matmul(former, latter):
    return jnp.dot(former, latter, preferred_element_type=jnp.float32)


def unchanged(status):
    return status


def document_ids(lengths, positions):
    bounds = jnp.cumsum(lengths, axis=1)
    return jnp.sum((positions[None, :, None] >= bounds[:, None, :]).astype(jnp.int32), axis=2)


def block_mask(lengths, query_block, key_block, block_span):
    offsets = jnp.arange(block_span, dtype=jnp.int32)
    query_pos = query_block * block_span + offsets
    key_pos = key_block * block_span + offsets
    query_docs = document_ids(lengths, query_pos)
    key_docs = document_ids(lengths, key_pos)
    causal = key_pos[None, None, :] <= query_pos[None, :, None]
    return causal & (key_docs[:, None, :] == query_docs[:, :, None])


def block_scores(query_heads, key_heads, mix_pre, visible):
    scaled = jnp.einsum(
        "rqhd,rkhd->rhqk", query_heads, key_heads, preferred_element_type=jnp.float32
    ) * HEAD_DIM ** (-0.5)
    mixed_scores = jnp.einsum("rhqk,hg->rgqk", scaled, mix_pre, precision=PRECISE)
    return (scaled, jnp.where(visible[:, None], mixed_scores, MASKED))


def block_probs(mixed_scores, log_total, visible):
    return jnp.where(visible[:, None], jnp.exp(mixed_scores - log_total[..., None]), 0.0)


def grad_block(
    query_heads,
    grad_heads,
    log_total,
    row_delta,
    key_heads,
    value_heads,
    visible,
    mix_pre,
    mix_post,
):
    scaled, mixed_scores = block_scores(query_heads, key_heads, mix_pre, visible)
    soft_weights = block_probs(mixed_scores, log_total, visible)
    post_mix = jnp.einsum("rgqk,gh->rhqk", soft_weights, mix_post, precision=PRECISE).astype(
        jnp.bfloat16
    )
    post_grads = jnp.einsum(
        "rqhd,rkhd->rhqk", grad_heads, value_heads, preferred_element_type=jnp.float32
    )
    soft_grads = jnp.einsum("rhqk,gh->rgqk", post_grads, mix_post, precision=PRECISE)
    post_mix_grad = jnp.einsum("rgqk,rhqk->gh", soft_weights, post_grads, precision=PRECISE)
    mixed_grads = soft_weights * (soft_grads - row_delta[..., None])
    pre_mix_grad = jnp.einsum("rhqk,rgqk->hg", scaled, mixed_grads, precision=PRECISE)
    score_grads = jnp.einsum("rgqk,hg->rhqk", mixed_grads, mix_pre, precision=PRECISE).astype(
        jnp.bfloat16
    )
    query_grad = jnp.einsum(
        "rhqk,rkhd->rqhd", score_grads, key_heads, preferred_element_type=jnp.float32
    ) * HEAD_DIM ** (-0.5)
    key_grad = jnp.einsum(
        "rhqk,rqhd->rkhd", score_grads, query_heads, preferred_element_type=jnp.float32
    ) * HEAD_DIM ** (-0.5)
    value_grad = jnp.einsum(
        "rhqk,rqhd->rkhd", post_mix, grad_heads, preferred_element_type=jnp.float32
    )
    return (query_grad, key_grad, value_grad, pre_mix_grad, post_mix_grad)


def travel(moving, totals, update, sender, turns):

    def advance(offset, carried):
        current, status = carried
        status = update(offset, current, status)
        return (sender(current), status)

    current, status = lax.fori_loop(0, turns - 1, advance, (moving, totals))
    return update(turns - 1, current, status)


def shards(
    inputs,
    doc_lengths,
    norm1_gain,
    w_query,
    w_key,
    w_value,
    head_mix_pre,
    head_mix_post,
    w_attn_out,
    norm2_gain,
    w_ff_in,
    w_ff_out,
    out_cotangent,
):
    row_count, block_span, model_width = inputs.shape
    head_count = head_mix_pre.shape[0]
    head_size = model_width // head_count
    circle = lax.axis_size("blk")
    own_block = lax.axis_index("blk")
    tokens_flat = inputs.reshape(row_count * block_span, model_width).astype(jnp.float32)
    normed_one, pull_one = jax.vjp(rms_norm, tokens_flat, norm1_gain)
    normed_low = normed_one.astype(jnp.bfloat16)

    def heads_of(weight):
        return (
            matmul(normed_low, weight)
            .astype(jnp.bfloat16)
            .reshape(row_count, block_span, head_count, head_size)
        )

    query_heads = heads_of(w_query)
    key_heads = heads_of(w_key)
    value_heads = heads_of(w_value)
    key_value = jnp.stack((key_heads, value_heads))

    def run_pair(totals, update):
        return travel(
            key_value, totals, update, lambda current: from_behind(current, "blk", 1), circle
        )

    def mask_for(query_block, key_block):
        return block_mask(doc_lengths, query_block, key_block, block_span)

    def total_update(offset, current, totals):
        visible = mask_for(own_block, (own_block - offset) % circle)

        def total_compute(status):
            running_top, running_mass = status
            scaled, mixed_scores = block_scores(query_heads, current, head_mix_pre, visible)
            new_top = jnp.maximum(running_top, jnp.max(mixed_scores, axis=3))
            shifted = jnp.where(visible[:, None], jnp.exp(mixed_scores - new_top[..., None]), 0.0)
            return (
                new_top,
                running_mass * jnp.exp(running_top - new_top) + jnp.sum(shifted, axis=3),
            )

        return lax.cond(jnp.any(visible), total_compute, unchanged, totals)

    stat_shape = (row_count, head_count, block_span)
    running_top, running_mass = travel(
        key_heads,
        (jnp.full(stat_shape, MASKED, jnp.float32), jnp.zeros(stat_shape, jnp.float32)),
        total_update,
        lambda current: from_behind(current, "blk", 1),
        circle,
    )
    log_total = running_top + jnp.log(running_mass)

    def output_update(offset, current, totals):
        visible = mask_for(own_block, (own_block - offset) % circle)

        def output_compute(status):
            scaled, mixed_scores = block_scores(query_heads, current[0], head_mix_pre, visible)
            soft_weights = block_probs(mixed_scores, log_total, visible)
            post_mix = jnp.einsum(
                "rgqk,gh->rhqk", soft_weights, head_mix_post, precision=PRECISE
            ).astype(jnp.bfloat16)
            return status + jnp.einsum(
                "rhqk,rkhd->rqhd", post_mix, current[1], preferred_element_type=jnp.float32
            )

        return lax.cond(jnp.any(visible), output_compute, unchanged, totals)

    head_shape = (row_count, block_span, head_count, head_size)
    attended_sum = run_pair(jnp.zeros(head_shape, jnp.float32), output_update)
    attended = attended_sum.reshape(row_count * block_span, model_width).astype(jnp.bfloat16)
    middle = tokens_flat + matmul(attended, w_attn_out)
    normed_two, pull_two = jax.vjp(rms_norm, middle, norm2_gain)
    normed_two_low = normed_two.astype(jnp.bfloat16)
    hidden = matmul(normed_two_low, w_ff_in)
    active, pull_gelu = jax.vjp(jax.nn.gelu, hidden)
    active_low = active.astype(jnp.bfloat16)
    output = (
        (middle + matmul(active_low, w_ff_out))
        .astype(jnp.bfloat16)
        .reshape(row_count, block_span, model_width)
    )
    cotangent = out_cotangent.reshape(row_count * block_span, model_width)
    grad_ff_out = matmul(active_low.T, cotangent)
    d_active = matmul(cotangent, w_ff_out.T)
    d_hidden = pull_gelu(d_active)[0].astype(jnp.bfloat16)
    grad_ff_in = matmul(normed_two_low.T, d_hidden)
    d_normed_two = matmul(d_hidden, w_ff_in.T)
    d_middle_norm, grad_gain_two = pull_two(d_normed_two)
    d_middle = cotangent.astype(jnp.float32) + d_middle_norm
    d_branch = d_middle.astype(jnp.bfloat16)
    grad_attn_out = matmul(attended.T, d_branch)
    grad_heads = matmul(d_branch, w_attn_out.T).astype(jnp.bfloat16).reshape(head_shape)

    def delta_update(offset, current, totals):
        visible = mask_for(own_block, (own_block - offset) % circle)

        def delta_compute(status):
            scaled, mixed_scores = block_scores(query_heads, current[0], head_mix_pre, visible)
            soft_weights = block_probs(mixed_scores, log_total, visible)
            post_grads = jnp.einsum(
                "rqhd,rkhd->rhqk", grad_heads, current[1], preferred_element_type=jnp.float32
            )
            soft_grads = jnp.einsum("rhqk,gh->rgqk", post_grads, head_mix_post, precision=PRECISE)
            return status + jnp.sum(soft_weights * soft_grads, axis=3)

        return lax.cond(jnp.any(visible), delta_compute, unchanged, totals)

    row_delta = run_pair(jnp.zeros(stat_shape, jnp.float32), delta_update)
    mix_zero = jnp.zeros((head_count, head_count), jnp.float32)
    heads_zero = jnp.zeros(head_shape, jnp.float32)

    def key_update(offset, current, accumulated):
        visible = mask_for(own_block, (own_block - offset) % circle)

        def key_compute(status):
            pair_grad, query_sum, pre_sum, post_sum = status
            d_query, d_key, d_value, d_pre, d_post = grad_block(
                query_heads,
                grad_heads,
                log_total,
                row_delta,
                current[0],
                current[1],
                visible,
                head_mix_pre,
                head_mix_post,
            )
            return (
                pair_grad + jnp.stack((d_key, d_value)),
                query_sum + d_query,
                pre_sum + d_pre,
                post_sum + d_post,
            )

        return lax.cond(jnp.any(visible), key_compute, unchanged, accumulated)

    def key_advance(offset, carried):
        current, accumulated = carried
        accumulated = key_update(offset, current, accumulated)
        arrived, arrived_grad = (
            from_behind_2(current, "blk", 1),
            from_behind_2(accumulated[0].astype(jnp.bfloat16), "blk", 1).astype(jnp.float32),
        )
        return (arrived, (arrived_grad, accumulated[1], accumulated[2], accumulated[3]))

    initial = (
        key_value,
        (jnp.zeros((2,) + head_shape, jnp.float32), heads_zero, mix_zero, mix_zero),
    )
    current, accumulated = lax.fori_loop(0, circle - 1, key_advance, initial)
    accumulated = key_update(circle - 1, current, accumulated)
    pair_grad = from_behind_2(accumulated[0].astype(jnp.bfloat16), "blk", 1).astype(jnp.float32)
    d_keys, d_values = (pair_grad[0], pair_grad[1])
    d_queries, pre_grad, post_grad = (accumulated[1], accumulated[2], accumulated[3])
    token_total = row_count * block_span
    d_queries_low = d_queries.reshape(token_total, model_width).astype(jnp.bfloat16)
    d_keys_low = d_keys.reshape(token_total, model_width).astype(jnp.bfloat16)
    d_values_low = d_values.reshape(token_total, model_width).astype(jnp.bfloat16)
    grad_query = matmul(normed_low.T, d_queries_low)
    grad_key = matmul(normed_low.T, d_keys_low)
    grad_value = matmul(normed_low.T, d_values_low)
    d_normed_one = (
        matmul(d_queries_low, w_query.T)
        + matmul(d_keys_low, w_key.T)
        + matmul(d_values_low, w_value.T)
    )
    d_input_norm, grad_gain_one = pull_one(d_normed_one)
    input_grad = (
        (d_middle + d_input_norm).astype(jnp.bfloat16).reshape(row_count, block_span, model_width)
    )
    summed = (
        lax.psum_scatter(grad_gain_one, ("dp", "blk"), scatter_dimension=0, tiled=True),
        lax.psum_scatter(grad_query, ("dp", "blk"), scatter_dimension=0, tiled=True),
        lax.psum_scatter(grad_key, ("dp", "blk"), scatter_dimension=0, tiled=True),
        lax.psum_scatter(grad_value, ("dp", "blk"), scatter_dimension=0, tiled=True),
        lax.psum_scatter(grad_attn_out, ("dp", "blk"), scatter_dimension=0, tiled=True),
        lax.psum_scatter(grad_gain_two, ("dp", "blk"), scatter_dimension=0, tiled=True),
        lax.psum_scatter(grad_ff_in, ("dp", "blk"), scatter_dimension=0, tiled=True),
        lax.psum_scatter(grad_ff_out, ("dp", "blk"), scatter_dimension=0, tiled=True),
    )
    mixes = lax.psum((pre_grad, post_grad), ("dp", "blk"))
    return (
        output,
        input_grad,
        summed[0],
        summed[1],
        summed[2],
        summed[3],
        mixes[0],
        mixes[1],
        summed[4],
        summed[5],
        summed[6],
        summed[7],
    )


def solution(mesh):
    in_specs = (
        P("dp", "blk", None),
        P("dp", None),
        P(),
        P(),
        P(),
        P(),
        P(),
        P(),
        P(),
        P(),
        P(),
        P(),
        P("dp", "blk", None),
    )
    out_specs = (
        P("dp", "blk", None),
        P("dp", "blk", None),
        P(("dp", "blk")),
        P(("dp", "blk"), None),
        P(("dp", "blk"), None),
        P(("dp", "blk"), None),
        P(),
        P(),
        P(("dp", "blk"), None),
        P(("dp", "blk")),
        P(("dp", "blk"), None),
        P(("dp", "blk"), None),
    )
    return jax.shard_map(shards, mesh=mesh, in_specs=in_specs, out_specs=out_specs, check_vma=False)
```

profile of v0, /device:TPU:0, one launch (start us, length us, event | category | flops | bytes accessed | tf_op | source)
XLA Modules:
  0.0 4465.0 jit_solution(5330649070494756283)
XLA Ops:
  61.5 258.5 %while.89 = (s32[]{:T(128)}, bf16[2,512,12,64]{1,3,2,0:T(8,128)(2,1)}, f32[2,12,512]{1,2,0:T(8,128)}, f32[2,12,512]{1,2,0:T(8,128)}, s32[]{:T(128)}, /*index=5*/...) while((s32[]{:T(128)}, ...), condition=%wide.region_13.14_spmd, body=%wide.region_5.13_spmd.sunk | while | flops 1757223936 | bytes 116601968 | solution.py:110
  84.4 109.3 %conditional.17 = ((f32[2,12,512]{1,2,0:T(8,128)}, f32[2,12,512]{1,2,0:T(8,128)})) conditional(s32[]{:T(128)} %convert_element_type.403, (f32[2,12,512]{1,2,0:T(8,128)}, f32[2,12,512]{1,2,0:T(8,128)}) %tuple.307, (pred[2,512,512]{2,1,0:T(8,128)(4,1)S(1)}, bf16[2,512,12,64]{1,3,2,0:T(8,128)(2,1)S(1)}, bf16[2,512,12,64]{1,3,2,0:T(8,128)(2,1)}, ...), branch_computations={%region_9.9_spmd, %region_10.12_spmd} | conditional | flops 1755340800 | bytes 106087088 | solution.py:171
  84.5 11.5 broadcast_multiply_fusion
  96.0 78.3 %bitcast_reduce_fusion = (f32[2,12,512]{1,2,0:T(8,128)S(1)}, f32[2,512,512,12]{2,3,1,0:T(8,128)}) fusion(pred[2,512,512]{2,1,0:T(8,128)(4,1)S(1)} %get-tuple-element.1201, f32[12,12]{0,1:T(8,128)S(1)} %get-tuple-element.1204, f32[2,12,512,512]{3,2,1,0:T(8,128)} %broadcast_multiply_fusion), kind=kOutput, calls=%fused_computation.1 | convolution fusion | flops 918540288 | bytes 50905664 | tf_op jit(solution)/shard_map/while/body/eval_jaxpr/cond/branch_1_fun/rhqk,hg->rgqk/dot_general | solution.py:57
  174.4 18.0 fusion.2
  206.1 111.2 %collective-permute-start = (bf16[2,512,12,64]{1,3,2,0:T(8,128)(2,1)}, bf16[2,512,12,64]{1,3,2,0:T(8,128)(2,1)}, u32[]{:S(2)}, u32[]{:S(2)}) collective-permute-start(bf16[2,512,12,64]{1,3,2,0:T(8,128)(2,1)} %copy.443), channel_id=1, source_target_pairs={{0,1},{1,2},{2,3},{4,5},{5,6},{6,7},{8,9},{9,10},{10,11},{12,13},{... | collective-permute-start | bytes 4718600 | tf_op jit(solution)/shard_map/while/body/eval_jaxpr/ppermute | solution.py:17
  320.0 33.7 conditional.8
  357.9 493.6 %while.90 = (s32[]{:T(128)}, bf16[2,2,512,12,64]{2,4,3,1,0:T(8,128)(2,1)}, f32[2,512,12,64]{1,3,2,0:T(8,128)}, s32[]{:T(128)}, s32[]{:T(128)}, /*index=5*/s32[2,...) while((s32[]{:T(128)}, ...), condition=%wide.region_24.25_spmd, body=%wide.region_18.24_spmd.sunk | while | flops 3456678912 | bytes 161560144 | solution.py:110
  361.9 17.7 collective-permute-start.1
  382.6 137.1 %conditional.18 = (f32[2,512,12,64]{1,3,2,0:T(8,128)}) conditional(s32[]{:T(128)} %convert_element_type.405, f32[2,512,12,64]{1,3,2,0:T(8,128)} %get-tuple-element.2284, (pred[2,512,512]{2,1,0:T(8,128)(4,1)}, bf16[2,2,512,12,64]{2,4,3,1,0:T(8,128)(2,1)}, bf16[2,512,12,64]{1,3,2,0:T(8,128)(2,1)S(1)}, f32[12,12]{0,1:T(8,128)S(1)}, ...), branch_computations={%region_22.22_spmd, %region_23.23_spmd} | conditional | flops 3454795776 | bytes 141608064 | solution.py:196
  382.6 11.5 broadcast_multiply_fusion.2
  394.1 59.0 %fusion.17 = f32[2,512,512,12]{2,3,1,0:T(8,128)} fusion(f32[2,12,512,512]{3,2,1,0:T(8,128)} %broadcast_multiply_fusion.2, f32[12,12]{0,1:T(8,128)S(1)} %get-tuple-element.1228), kind=kOutput, calls=%fused_computation.31 | convolution fusion | flops 905969664 | bytes 50332224 | tf_op jit(solution)/shard_map/while/body/eval_jaxpr/cond/branch_1_fun/rhqk,hg->rgqk/dot_general | solution.py:57
  453.1 50.4 %convert_bitcast_fusion = bf16[2,12,512,512]{3,1,2,0:T(8,128)(2,1)} fusion(f32[2,512,512,12]{2,3,1,0:T(8,128)} %fusion.17, f32[2,12,512]{1,2,0:T(8,128)} %get-tuple-element.1229, pred[2,512,512]{2,1,0:T(8,128)(4,1)} %get-tuple-element.1225, f32[12,12]{0,1:T(8,128)S(1)} %get-tuple-element.1230), kind=kOutput, calls=%fused_computation.34 | convolution fusion | flops 931135488 | bytes 38322752 | tf_op jit(solution)/shard_map/while/body/eval_jaxpr/cond/branch_1_fun/rgqk,gh->rhqk/dot_general | solution.py:189
  503.5 16.1 bitcast_add_fusion
  523.5 95.9 %collective-permute-start.1 = (bf16[2,2,512,12,64]{2,4,3,1,0:T(8,128)(2,1)}, bf16[2,2,512,12,64]{2,4,3,1,0:T(8,128)(2,1)}, u32[]{:S(2)}, u32[]{:S(2)}) collective-permute-start(bf16[2,2,512,12,64]{2,4,3,1,0:T(8,128)(2,1)} %copy.458), channel_id=1, source_target_pairs={{0,1},{1,2},{2,3},{4,5},{5,6},{6,7},{8,9},{9,10},{10,11},{12,13},{... | collective-permute-start | bytes 9437192 | tf_op jit(solution)/shard_map/while/body/eval_jaxpr/ppermute | solution.py:17
  627.4 219.7 %collective-permute-start.1 = (bf16[2,2,512,12,64]{2,4,3,1,0:T(8,128)(2,1)}, bf16[2,2,512,12,64]{2,4,3,1,0:T(8,128)(2,1)}, u32[]{:S(2)}, u32[]{:S(2)}) collective-permute-start(bf16[2,2,512,12,64]{2,4,3,1,0:T(8,128)(2,1)} %copy.458), channel_id=1, source_target_pairs={{0,1},{1,2},{2,3},{4,5},{5,6},{6,7},{8,9},{9,10},{10,11},{12,13},{... | collective-permute-start | bytes 9437192 | tf_op jit(solution)/shard_map/while/body/eval_jaxpr/ppermute | solution.py:17
  851.5 11.9 conditional.9
  869.6 10.5 fusion.252
  880.2 15.4 fusion.233
  895.5 8.3 multiply_reduce_fusion
  927.4 633.4 %while.91 = (s32[]{:T(128)}, bf16[2,2,512,12,64]{2,4,3,1,0:T(8,128)(2,1)}, f32[2,12,512]{1,2,0:T(8,128)S(1)}, s32[]{:T(128)}, s32[]{:T(128)}, /*index=5*/s32[2,1...) while((s32[]{:T(128)}, ...), condition=%wide.region_36.37_spmd, body=%wide.region_29.36_spmd.sunk | while | flops 3462183936 | bytes 184301168 | solution.py:110
  953.5 32.5 collective-permute-start.2
  988.9 162.3 %conditional.19 = (f32[2,12,512]{1,2,0:T(8,128)S(1)}) conditional(s32[]{:T(128)} %convert_element_type.407, f32[2,12,512]{1,2,0:T(8,128)S(1)} %get-tuple-element.2330, (pred[2,512,512]{2,1,0:T(8,128)(4,1)}, bf16[2,2,512,12,64]{2,4,3,1,0:T(8,128)(2,1)}, bf16[2,512,12,64]{1,3,2,0:T(8,128)(2,1)S(1)}, f32[12,12]{0,1:T(8,128)S(1)}, ...), branch_computations={%region_33.33_spmd, %region_34.35_spmd} | conditional | flops 3460300800 | bytes 164349088 | solution.py:236
  989.0 11.6 broadcast_multiply_fusion.4
  1000.6 11.6 fusion.75
  1012.2 59.1 %fusion.69 = f32[2,512,512,12]{2,3,1,0:T(8,128)} fusion(f32[2,12,512,512]{3,2,1,0:T(8,128)} %fusion.75, f32[12,12]{1,0:T(8,128)S(1)} %get-tuple-element.1256), kind=kOutput, calls=%fused_computation.89 | convolution fusion | flops 905969664 | bytes 50332224 | tf_op jit(solution)/shard_map/while/body/eval_jaxpr/cond/branch_1_fun/rhqk,gh->rgqk/dot_general | solution.py:233
  1071.3 78.8 %fusion.66 = f32[2,12,512]{1,2,0:T(8,128)} fusion(f32[2,512,512,12]{2,3,1,0:T(8,128)} %fusion.69, f32[2,12,512,512]{3,2,1,0:T(8,128)} %broadcast_multiply_fusion.4, f32[2,12,512]{1,2,0:T(8,128)} %get-tuple-element.1254, pred[2,512,512]{2,1,0:T(8,128)(4,1)} %get-tuple-element.1250, f32[12,12]{0,1:T(8,128)S(1)} %get-tuple-element.1253), kind=kOutput, calls=%fused_computation.85 | convolution fusion | flops 937414656 | bytes 50954816 | tf_op jit(solution)/shard_map/while/body/eval_jaxpr/cond/branch_1_fun/rhqk,hg->rgqk/dot_general | solution.py:57
  1155.1 107.5 %collective-permute-start.2 = (bf16[2,2,512,12,64]{2,4,3,1,0:T(8,128)(2,1)}, bf16[2,2,512,12,64]{2,4,3,1,0:T(8,128)(2,1)}, u32[]{:S(2)}, u32[]{:S(2)}) collective-permute-start(bf16[2,2,512,12,64]{2,4,3,1,0:T(8,128)(2,1)} %copy.469), channel_id=1, source_target_pairs={{0,1},{1,2},{2,3},{4,5},{5,6},{6,7},{8,9},{9,10},{10,11},{12,13},{... | collective-permute-start | bytes 9437192 | tf_op jit(solution)/shard_map/while/body/eval_jaxpr/ppermute | solution.py:17
  1270.4 286.0 %collective-permute-start.2 = (bf16[2,2,512,12,64]{2,4,3,1,0:T(8,128)(2,1)}, bf16[2,2,512,12,64]{2,4,3,1,0:T(8,128)(2,1)}, u32[]{:S(2)}, u32[]{:S(2)}) collective-permute-start(bf16[2,2,512,12,64]{2,4,3,1,0:T(8,128)(2,1)} %copy.469), channel_id=1, source_target_pairs={{0,1},{1,2},{2,3},{4,5},{5,6},{6,7},{8,9},{9,10},{10,11},{12,13},{... | collective-permute-start | bytes 9437192 | tf_op jit(solution)/shard_map/while/body/eval_jaxpr/ppermute | solution.py:17
  1560.8 10.8 conditional.10
  1573.7 1840.6 %while.92 = (s32[]{:T(128)}, bf16[2,2,512,12,64]{2,4,3,1,0:T(8,128)(2,1)}, f32[2,2,512,12,64]{2,4,3,1,0:T(8,128)}, f32[2,512,12,64]{1,3,2,0:T(8,128)}, f32[12,12...) while((s32[]{:T(128)}, ...), condition=%wide.region_46.47_spmd.clone, body=%wide.region_40.0_spmd.clone.sunk | while | flops 9524788224 | bytes 560072448 | solution.py:280
  1587.1 422.4 %conditional.20 = ((f32[2,2,512,12,64]{2,4,3,1,0:T(8,128)}, f32[2,512,12,64]{1,3,2,0:T(8,128)}, f32[12,12]{1,0:T(8,128)S(1)}, f32[12,12]{1,0:T(8,128)S(1)})) conditional(s32[]{:T(128)} %convert_element_type.409, (f32[2,2,512,12,64]{2,4,3,1,0:T(8,128)}, f32[2,512,12,64]{1,3,2,0:T(8,128)}, f32[12,12]{1,0:T(8,128)S(1)}, ...), branch_computations={%region_44.44_spmd, %region_45.45_spmd} | conditional | flops 9518186496 | bytes 470913696 | solution.py:265
  1587.1 11.6 broadcast_multiply_fusion.6
  1598.7 11.6 fusion.130
  1610.4 75.7 %fusion.102 = f32[2,12,512,512]{3,1,2,0:T(8,128)} fusion(f32[2,12,512,512]{3,2,1,0:T(8,128)} %broadcast_multiply_fusion.6, f32[2,12,512]{1,2,0:T(8,128)} %get-tuple-element.1282, pred[2,512,512]{2,1,0:T(8,128)(4,1)S(1)} %copy-done.5, f32[12,12]{1,0:T(8,128)S(1)} %get-tuple-element.1281), kind=kOutput, calls=%fused_computation.130 | convolution fusion | flops 924844032 | bytes 50905664 | tf_op jit(solution)/shard_map/while/body/eval_jaxpr/cond/branch_1_fun/rhqk,hg->rgqk/dot_general | solution.py:57
  1686.0 53.2 %fusion.147 = f32[12,12]{1,0:T(8,128)S(1)} fusion(f32[12,12]{1,0:T(8,128)S(1)} %get-tuple-element.1288, f32[2,12,512,512]{3,2,1,0:T(8,128)} %fusion.130, f32[2,12,512,512]{3,1,2,0:T(8,128)} %fusion.102), kind=kOutput, calls=%fused_computation.163 | convolution fusion | flops 905969792 | bytes 50332800 | tf_op jit(solution)/shard_map/while/body/eval_jaxpr/cond/branch_1_fun/rgqk,rhqk->gh/dot_general | solution.py:85
  1739.3 80.9 %fusion.100 = f32[2,12,512,512]{3,1,2,0:T(8,128)} fusion(f32[2,12,512,512]{3,1,2,0:T(8,128)} %fusion.102, f32[2,12,512,512]{3,2,1,0:T(8,128)} %fusion.130, f32[2,12,512]{1,2,0:T(8,128)S(1)} %get-tuple-element.1285, f32[12,12]{0,1:T(8,128)S(1)} %get-tuple-element.1284), kind=kOutput, calls=%fused_computation.127 | convolution fusion | flops 918552576 | bytes 75547200 | tf_op jit(solution)/shard_map/while/body/eval_jaxpr/cond/branch_1_fun/rhqk,gh->rgqk/dot_general | solution.py:84
  1820.1 53.7 %fusion.152 = f32[12,12]{1,0:T(8,128)S(1)} fusion(f32[12,12]{1,0:T(8,128)S(1)} %get-tuple-element.1287, f32[2,12,512,512]{3,1,2,0:T(8,128)} %fusion.100, f32[2,12,512,512]{3,2,1,0:T(8,128)} %broadcast_multiply_fusion.6), kind=kOutput, calls=%fused_computation.164 | convolution fusion | flops 905969792 | bytes 50332800 | tf_op jit(solution)/shard_map/while/body/eval_jaxpr/cond/branch_1_fun/rhqk,rgqk->hg/dot_general | solution.py:87
  1873.8 45.3 %convert_bitcast_fusion.2 = bf16[2,12,512,512]{3,1,2,0:T(8,128)(2,1)} fusion(f32[2,12,512,512]{3,1,2,0:T(8,128)} %fusion.102, f32[12,12]{0,1:T(8,128)S(1)} %get-tuple-element.1284), kind=kOutput, calls=%fused_computation.141 | convolution fusion | flops 912261120 | bytes 37749312 | tf_op jit(solution)/shard_map/while/body/eval_jaxpr/cond/branch_1_fun/rgqk,gh->rhqk/dot_general | solution.py:78
  1919.1 45.8 %convert_bitcast_fusion.3 = bf16[2,12,512,512]{3,1,2,0:T(8,128)(2,1)} fusion(f32[2,12,512,512]{3,1,2,0:T(8,128)} %fusion.100, f32[12,12]{1,0:T(8,128)S(1)} %get-tuple-element.1281), kind=kOutput, calls=%fused_computation.142 | convolution fusion | flops 912261120 | bytes 37749312 | tf_op jit(solution)/shard_map/while/body/eval_jaxpr/cond/branch_1_fun/rgqk,hg->rhqk/dot_general | solution.py:88
  1964.9 11.2 fusion.123
  1976.1 14.5 bitcast_add_fusion.2
  1990.6 11.7 multiply_bitcast_fusion
  2002.3 7.0 maximum_add_fusion
  2014.5 28.9 collective-permute-start.4
  2043.4 130.8 %collective-permute-start.3 = (bf16[2,2,512,12,64]{2,4,3,1,0:T(8,128)(2,1)}, bf16[2,2,512,12,64]{2,4,3,1,0:T(8,128)(2,1)}, u32[]{:S(2)}, u32[]{:S(2)}) collective-permute-start(bf16[2,2,512,12,64]{2,4,3,1,0:T(8,128)(2,1)} %copy.483), channel_id=1, source_target_pairs={{0,1},{1,2},{2,3},{3,0},{4,5},{5,6},{6,7},{7,4},{8,9},{9,10},{10,1... | collective-permute-start | bytes 9437192 | tf_op jit(solution)/shard_map/while/body/eval_jaxpr/ppermute | solution.py:22
  2174.2 187.0 %collective-permute-done.4 = bf16[2,2,512,12,64]{2,4,3,1,0:T(8,128)(2,1)} collective-permute-done((bf16[2,2,512,12,64]{2,4,3,1,0:T(8,128)(2,1)}, bf16[2,2,512,12,64]{2,4,3,1,0:T(8,128)(2,1)}, u32[]{:S(2)}, u32[]{:S(2)}) %collective-permute-start.4) | collective-permute-done | bytes 3145760 | tf_op jit(solution)/shard_map/while/body/eval_jaxpr/ppermute | solution.py:22
  2366.6 28.3 collective-permute-done.3
  2411.4 388.4 %collective-permute-start.4 = (bf16[2,2,512,12,64]{2,4,3,1,0:T(8,128)(2,1)}, bf16[2,2,512,12,64]{2,4,3,1,0:T(8,128)(2,1)}, u32[]{:S(2)}, u32[]{:S(2)}) collective-permute-start(bf16[2,2,512,12,64]{2,4,3,1,0:T(8,128)(2,1)} %convert_element_type.410), channel_id=1, source_target_pairs={{0,1},{1,2},{2,3},{3,0},{4,5},{5,6},{6,7},{7,4},{8,9},{9,10},{10,1... | collective-permute-start | bytes 9437192 | tf_op jit(solution)/shard_map/while/body/eval_jaxpr/ppermute | solution.py:22
  2802.2 66.0 %collective-permute-done.4 = bf16[2,2,512,12,64]{2,4,3,1,0:T(8,128)(2,1)} collective-permute-done((bf16[2,2,512,12,64]{2,4,3,1,0:T(8,128)(2,1)}, bf16[2,2,512,12,64]{2,4,3,1,0:T(8,128)(2,1)}, u32[]{:S(2)}, u32[]{:S(2)}) %collective-permute-start.4) | collective-permute-done | bytes 3145760 | tf_op jit(solution)/shard_map/while/body/eval_jaxpr/ppermute | solution.py:22
  2873.6 28.3 collective-permute-done.3
  2917.9 393.8 %collective-permute-start.3 = (bf16[2,2,512,12,64]{2,4,3,1,0:T(8,128)(2,1)}, bf16[2,2,512,12,64]{2,4,3,1,0:T(8,128)(2,1)}, u32[]{:S(2)}, u32[]{:S(2)}) collective-permute-start(bf16[2,2,512,12,64]{2,4,3,1,0:T(8,128)(2,1)} %copy.483), channel_id=1, source_target_pairs={{0,1},{1,2},{2,3},{3,0},{4,5},{5,6},{6,7},{7,4},{8,9},{9,10},{10,1... | collective-permute-start | bytes 9437192 | tf_op jit(solution)/shard_map/while/body/eval_jaxpr/ppermute | solution.py:22
  3311.7 63.5 %collective-permute-done.4 = bf16[2,2,512,12,64]{2,4,3,1,0:T(8,128)(2,1)} collective-permute-done((bf16[2,2,512,12,64]{2,4,3,1,0:T(8,128)(2,1)}, bf16[2,2,512,12,64]{2,4,3,1,0:T(8,128)(2,1)}, u32[]{:S(2)}, u32[]{:S(2)}) %collective-permute-start.4) | collective-permute-done | bytes 3145760 | tf_op jit(solution)/shard_map/while/body/eval_jaxpr/ppermute | solution.py:22
  3380.7 28.3 collective-permute-done.3
  3414.3 15.4 conditional.11
  3440.4 457.4 %collective-permute-done.5 = bf16[2,2,512,12,64]{2,4,3,1,0:T(8,128)(2,1)} collective-permute-done((bf16[2,2,512,12,64]{2,4,3,1,0:T(8,128)(2,1)}, bf16[2,2,512,12,64]{2,4,3,1,0:T(8,128)(2,1)}, u32[]{:S(2)}, u32[]{:S(2)}) %collective-permute-start.5) | collective-permute-done | bytes 3145760 | tf_op jit(solution)/shard_map/ppermute | solution.py:22
  3915.2 12.8 fusion.253
  3928.7 10.7 fusion.251
  3942.8 12.8 add_convert_fusion
  3961.1 39.8 all-reduce.2
  4007.0 63.2 %reduce-scatter.9.cloned.1.call-done = f32[24,768]{1,0:T(8,128)} async-done(((f32[768,768]{1,0:T(8,128)}), f32[24,768]{1,0:T(8,128)}) %reduce-scatter.9.cloned.1.call-update) | async-done | bytes 73744 | tf_op jit(solution)/shard_map/reduce_scatter | solution.py:304
  4070.3 104.7 %reduce-scatter.11.cloned.1.call-done = f32[24,768]{1,0:T(8,128)} async-done(((f32[768,768]{1,0:T(8,128)}), f32[24,768]{1,0:T(8,128)}) %reduce-scatter.11.cloned.1.call-update) | async-done | bytes 73744 | tf_op jit(solution)/shard_map/reduce_scatter | solution.py:305
  4174.9 141.0 %reduce-scatter.17.cloned.1.call-done = f32[96,768]{1,0:T(8,128)} async-done(((f32[3072,768]{1,0:T(8,128)}), f32[96,768]{1,0:T(8,128)}) %reduce-scatter.17.cloned.1.call-update) | async-done | bytes 294928 | tf_op jit(solution)/shard_map/reduce_scatter | solution.py:309
  4315.9 142.0 %reduce-scatter.15.cloned.1.call-done = f32[24,3072]{1,0:T(8,128)} async-done(((f32[768,3072]{1,0:T(8,128)}), f32[24,3072]{1,0:T(8,128)}) %reduce-scatter.15.cloned.1.call-update) | async-done | bytes 294928 | tf_op jit(solution)/shard_map/reduce_scatter | solution.py:308
  (322 shorter events, 266.6 us)
Async XLA Ops:
  7.2 29.4 copy-start
  7.2 6.2 copy-start.64
  7.2 3999.8 %reduce-scatter.13.cloned.1.call-start = ((), (), s32[]{:S(2)}) async-start(), calls=%async_computation.9 | async-start | bytes 2433024 | tf_op jit(solution)/shard_map/reduce_scatter | solution.py:306
  17.7 4.8 copy-start.62
  17.7 4.9 copy-start.30
  17.7 5.0 copy-start.46
  61.5 258.5 %copy-start.31 = (f32[12,12]{1,0:T(8,128)S(1)}, f32[12,12]{1,0:T(8,128)}, u32[]{:S(2)}) copy-start(f32[12,12]{1,0:T(8,128)} %param.43) | copy-start | bytes 1732
  78.7 115.1 %collective-permute-start = (bf16[2,512,12,64]{1,3,2,0:T(8,128)(2,1)}, bf16[2,512,12,64]{1,3,2,0:T(8,128)(2,1)}, u32[]{:S(2)}, u32[]{:S(2)}) collective-permute-start(bf16[2,512,12,64]{1,3,2,0:T(8,128)(2,1)} %copy.443), channel_id=1, source_target_pairs={{0,1},{1,2},{2,3},{4,5},{5,6},{6,7},{8,9},{9,10},{10,11},{12,13},{... | collective-permute-start | bytes 4718600 | tf_op jit(solution)/shard_map/while/body/eval_jaxpr/ppermute | solution.py:17
  96.0 78.3 %copy-start.6 = (f32[2,12,512]{1,2,0:T(8,128)S(1)}, f32[2,12,512]{1,2,0:T(8,128)}, u32[]{:S(2)}) copy-start(f32[2,12,512]{1,2,0:T(8,128)} %get-tuple-element.1200) | copy-start | bytes 147460 | tf_op jit(solution)/shard_map/while/body/eval_jaxpr/cond
  174.4 18.0 copy-start.13
  196.5 6.8 collective-permute-start
  206.1 113.5 %collective-permute-start = (bf16[2,512,12,64]{1,3,2,0:T(8,128)(2,1)}, bf16[2,512,12,64]{1,3,2,0:T(8,128)(2,1)}, u32[]{:S(2)}, u32[]{:S(2)}) collective-permute-start(bf16[2,512,12,64]{1,3,2,0:T(8,128)(2,1)} %copy.443), channel_id=1, source_target_pairs={{0,1},{1,2},{2,3},{4,5},{5,6},{6,7},{8,9},{9,10},{10,11},{12,13},{... | collective-permute-start | bytes 4718600 | tf_op jit(solution)/shard_map/while/body/eval_jaxpr/ppermute | solution.py:17
  353.7 4.2 copy-start.44
  357.9 493.7 %copy-start.18 = (pred[2,512,512]{2,1,0:T(8,128)(4,1)S(1)}, pred[2,512,512]{2,1,0:T(8,128)(4,1)}, u32[]{:S(2)}) copy-start(pred[2,512,512]{2,1,0:T(8,128)(4,1)} %get-tuple-element.1876) | copy-start | bytes 1572868
  357.9 493.7 %copy-start.32 = (f32[12,12]{1,0:T(8,128)S(1)}, f32[12,12]{1,0:T(8,128)}, u32[]{:S(2)}) copy-start(f32[12,12]{1,0:T(8,128)} %param.43) | copy-start | bytes 1732
  357.9 493.7 %copy-start.47 = (f32[12,12]{1,0:T(8,128)S(1)}, f32[12,12]{1,0:T(8,128)}, u32[]{:S(2)}) copy-start(f32[12,12]{1,0:T(8,128)} %param.44) | copy-start | bytes 1732
  361.9 157.7 %collective-permute-start.1 = (bf16[2,2,512,12,64]{2,4,3,1,0:T(8,128)(2,1)}, bf16[2,2,512,12,64]{2,4,3,1,0:T(8,128)(2,1)}, u32[]{:S(2)}, u32[]{:S(2)}) collective-permute-start(bf16[2,2,512,12,64]{2,4,3,1,0:T(8,128)(2,1)} %copy.458), channel_id=1, source_target_pairs={{0,1},{1,2},{2,3},{4,5},{5,6},{6,7},{8,9},{9,10},{10,11},{12,13},{... | collective-permute-start | bytes 9437192 | tf_op jit(solution)/shard_map/while/body/eval_jaxpr/ppermute | solution.py:17
  523.5 99.9 %collective-permute-start.1 = (bf16[2,2,512,12,64]{2,4,3,1,0:T(8,128)(2,1)}, bf16[2,2,512,12,64]{2,4,3,1,0:T(8,128)(2,1)}, u32[]{:S(2)}, u32[]{:S(2)}) collective-permute-start(bf16[2,2,512,12,64]{2,4,3,1,0:T(8,128)(2,1)} %copy.458), channel_id=1, source_target_pairs={{0,1},{1,2},{2,3},{4,5},{5,6},{6,7},{8,9},{9,10},{10,11},{12,13},{... | collective-permute-start | bytes 9437192 | tf_op jit(solution)/shard_map/while/body/eval_jaxpr/ppermute | solution.py:17
  627.4 223.8 %collective-permute-start.1 = (bf16[2,2,512,12,64]{2,4,3,1,0:T(8,128)(2,1)}, bf16[2,2,512,12,64]{2,4,3,1,0:T(8,128)(2,1)}, u32[]{:S(2)}, u32[]{:S(2)}) collective-permute-start(bf16[2,2,512,12,64]{2,4,3,1,0:T(8,128)(2,1)} %copy.458), channel_id=1, source_target_pairs={{0,1},{1,2},{2,3},{4,5},{5,6},{6,7},{8,9},{9,10},{10,11},{12,13},{... | collective-permute-start | bytes 9437192 | tf_op jit(solution)/shard_map/while/body/eval_jaxpr/ppermute | solution.py:17
  867.7 12.4 slice-start.4
  869.4 34.4 copy-start.28
  869.4 34.4 copy-start.57
  869.6 10.5 copy-start.43
  869.6 10.5 slice-start.5
  909.3 3097.7 %reduce-scatter.7.cloned.1.call-start = ((), (), s32[]{:S(2)}) async-start(), calls=%async_computation.6 | async-start | bytes 2433024 | tf_op jit(solution)/shard_map/reduce_scatter | solution.py:303
  927.4 633.4 %copy-start.33 = (f32[12,12]{1,0:T(8,128)S(1)}, f32[12,12]{1,0:T(8,128)}, u32[]{:S(2)}) copy-start(f32[12,12]{1,0:T(8,128)} %param.43) | copy-start | bytes 1732
  953.5 197.7 %collective-permute-start.2 = (bf16[2,2,512,12,64]{2,4,3,1,0:T(8,128)(2,1)}, bf16[2,2,512,12,64]{2,4,3,1,0:T(8,128)(2,1)}, u32[]{:S(2)}, u32[]{:S(2)}) collective-permute-start(bf16[2,2,512,12,64]{2,4,3,1,0:T(8,128)(2,1)} %copy.469), channel_id=1, source_target_pairs={{0,1},{1,2},{2,3},{4,5},{5,6},{6,7},{8,9},{9,10},{10,11},{12,13},{... | collective-permute-start | bytes 9437192 | tf_op jit(solution)/shard_map/while/body/eval_jaxpr/ppermute | solution.py:17
  989.0 11.6 copy-start.3
  1155.1 111.4 %collective-permute-start.2 = (bf16[2,2,512,12,64]{2,4,3,1,0:T(8,128)(2,1)}, bf16[2,2,512,12,64]{2,4,3,1,0:T(8,128)(2,1)}, u32[]{:S(2)}, u32[]{:S(2)}) collective-permute-start(bf16[2,2,512,12,64]{2,4,3,1,0:T(8,128)(2,1)} %copy.469), channel_id=1, source_target_pairs={{0,1},{1,2},{2,3},{4,5},{5,6},{6,7},{8,9},{9,10},{10,11},{12,13},{... | collective-permute-start | bytes 9437192 | tf_op jit(solution)/shard_map/while/body/eval_jaxpr/ppermute | solution.py:17
  1270.4 290.0 %collective-permute-start.2 = (bf16[2,2,512,12,64]{2,4,3,1,0:T(8,128)(2,1)}, bf16[2,2,512,12,64]{2,4,3,1,0:T(8,128)(2,1)}, u32[]{:S(2)}, u32[]{:S(2)}) collective-permute-start(bf16[2,2,512,12,64]{2,4,3,1,0:T(8,128)(2,1)} %copy.469), channel_id=1, source_target_pairs={{0,1},{1,2},{2,3},{4,5},{5,6},{6,7},{8,9},{9,10},{10,11},{12,13},{... | collective-permute-start | bytes 9437192 | tf_op jit(solution)/shard_map/while/body/eval_jaxpr/ppermute | solution.py:17
  1573.7 1840.6 %copy-start.48 = (f32[12,12]{1,0:T(8,128)S(1)}, f32[12,12]{1,0:T(8,128)}, u32[]{:S(2)}) copy-start(f32[12,12]{1,0:T(8,128)} %param.44) | copy-start | bytes 1732
  1576.0 7.1 copy-start.49
  1579.1 4.6 copy-start.1
  1587.1 11.6 copy-start.4
  1598.7 11.6 copy-start.5
  1964.9 11.2 copy-start.22
  1990.6 11.7 copy-start.23
  2014.5 346.7 %collective-permute-start.4 = (bf16[2,2,512,12,64]{2,4,3,1,0:T(8,128)(2,1)}, bf16[2,2,512,12,64]{2,4,3,1,0:T(8,128)(2,1)}, u32[]{:S(2)}, u32[]{:S(2)}) collective-permute-start(bf16[2,2,512,12,64]{2,4,3,1,0:T(8,128)(2,1)} %convert_element_type.410), channel_id=1, source_target_pairs={{0,1},{1,2},{2,3},{3,0},{4,5},{5,6},{6,7},{7,4},{8,9},{9,10},{10,1... | collective-permute-start | bytes 9437192 | tf_op jit(solution)/shard_map/while/body/eval_jaxpr/ppermute | solution.py:22
  2043.4 351.5 %collective-permute-start.3 = (bf16[2,2,512,12,64]{2,4,3,1,0:T(8,128)(2,1)}, bf16[2,2,512,12,64]{2,4,3,1,0:T(8,128)(2,1)}, u32[]{:S(2)}, u32[]{:S(2)}) collective-permute-start(bf16[2,2,512,12,64]{2,4,3,1,0:T(8,128)(2,1)} %copy.483), channel_id=1, source_target_pairs={{0,1},{1,2},{2,3},{3,0},{4,5},{5,6},{6,7},{7,4},{8,9},{9,10},{10,1... | collective-permute-start | bytes 9437192 | tf_op jit(solution)/shard_map/while/body/eval_jaxpr/ppermute | solution.py:22
  2174.2 220.7 %copy-start.50 = (s32[2,1,8]{2,0,1:T(2,128)S(1)}, s32[2,1,8]{2,0,1:T(2,128)}, u32[]{:S(2)}) copy-start(s32[2,1,8]{2,0,1:T(2,128)} %copy-done.49) | copy-start | bytes 196 | tf_op jit(solution)/shard_map/while
  2395.2 7.1 copy-start.49
  2398.3 4.6 copy-start.1
  2411.4 456.8 %collective-permute-start.4 = (bf16[2,2,512,12,64]{2,4,3,1,0:T(8,128)(2,1)}, bf16[2,2,512,12,64]{2,4,3,1,0:T(8,128)(2,1)}, u32[]{:S(2)}, u32[]{:S(2)}) collective-permute-start(bf16[2,2,512,12,64]{2,4,3,1,0:T(8,128)(2,1)} %convert_element_type.410), channel_id=1, source_target_pairs={{0,1},{1,2},{2,3},{3,0},{4,5},{5,6},{6,7},{7,4},{8,9},{9,10},{10,1... | collective-permute-start | bytes 9437192 | tf_op jit(solution)/shard_map/while/body/eval_jaxpr/ppermute | solution.py:22
  2799.8 102.2 %collective-permute-start.3 = (bf16[2,2,512,12,64]{2,4,3,1,0:T(8,128)(2,1)}, bf16[2,2,512,12,64]{2,4,3,1,0:T(8,128)(2,1)}, u32[]{:S(2)}, u32[]{:S(2)}) collective-permute-start(bf16[2,2,512,12,64]{2,4,3,1,0:T(8,128)(2,1)} %copy.483), channel_id=1, source_target_pairs={{0,1},{1,2},{2,3},{3,0},{4,5},{5,6},{6,7},{7,4},{8,9},{9,10},{10,1... | collective-permute-start | bytes 9437192 | tf_op jit(solution)/shard_map/while/body/eval_jaxpr/ppermute | solution.py:22
  2802.2 99.7 %copy-start.50 = (s32[2,1,8]{2,0,1:T(2,128)S(1)}, s32[2,1,8]{2,0,1:T(2,128)}, u32[]{:S(2)}) copy-start(s32[2,1,8]{2,0,1:T(2,128)} %copy-done.49) | copy-start | bytes 196 | tf_op jit(solution)/shard_map/while
  2901.9 7.1 copy-start.49
  2905.0 4.6 copy-start.1
  2917.9 457.4 %collective-permute-start.4 = (bf16[2,2,512,12,64]{2,4,3,1,0:T(8,128)(2,1)}, bf16[2,2,512,12,64]{2,4,3,1,0:T(8,128)(2,1)}, u32[]{:S(2)}, u32[]{:S(2)}) collective-permute-start(bf16[2,2,512,12,64]{2,4,3,1,0:T(8,128)(2,1)} %convert_element_type.410), channel_id=1, source_target_pairs={{0,1},{1,2},{2,3},{3,0},{4,5},{5,6},{6,7},{7,4},{8,9},{9,10},{10,1... | collective-permute-start | bytes 9437192 | tf_op jit(solution)/shard_map/while/body/eval_jaxpr/ppermute | solution.py:22
  2917.9 491.1 %collective-permute-start.3 = (bf16[2,2,512,12,64]{2,4,3,1,0:T(8,128)(2,1)}, bf16[2,2,512,12,64]{2,4,3,1,0:T(8,128)(2,1)}, u32[]{:S(2)}, u32[]{:S(2)}) collective-permute-start(bf16[2,2,512,12,64]{2,4,3,1,0:T(8,128)(2,1)} %copy.483), channel_id=1, source_target_pairs={{0,1},{1,2},{2,3},{3,0},{4,5},{5,6},{6,7},{7,4},{8,9},{9,10},{10,1... | collective-permute-start | bytes 9437192 | tf_op jit(solution)/shard_map/while/body/eval_jaxpr/ppermute | solution.py:22
  3311.7 97.2 %copy-start.50 = (s32[2,1,8]{2,0,1:T(2,128)S(1)}, s32[2,1,8]{2,0,1:T(2,128)}, u32[]{:S(2)}) copy-start(s32[2,1,8]{2,0,1:T(2,128)} %copy-done.49) | copy-start | bytes 196 | tf_op jit(solution)/shard_map/while
  3430.8 5.0 copy-start.12
  3430.8 5.0 copy-start.51
  3430.8 5.0 copy-start.56
  3435.9 462.0 %collective-permute-start.5 = (bf16[2,2,512,12,64]{2,4,3,1,0:T(8,128)(2,1)}, bf16[2,2,512,12,64]{2,4,3,1,0:T(8,128)(2,1)}, u32[]{:S(2)}, u32[]{:S(2)}) collective-permute-start(bf16[2,2,512,12,64]{2,4,3,1,0:T(8,128)(2,1)} %convert_element_type.309), channel_id=1, source_target_pairs={{0,1},{1,2},{2,3},{3,0},{4,5},{5,6},{6,7},{7,4},{8,9},{9,10},{10,1... | collective-permute-start | bytes 9437192 | tf_op jit(solution)/shard_map/ppermute | solution.py:22
  3440.4 629.9 %reduce-scatter.9.cloned.1.call-start = ((), (), s32[]{:S(2)}) async-start(), calls=%async_computation.7 | async-start | bytes 2433024 | tf_op jit(solution)/shard_map/reduce_scatter | solution.py:304
  3907.4 267.6 %reduce-scatter.11.cloned.1.call-start = ((), (), s32[]{:S(2)}) async-start(), calls=%async_computation.8 | async-start | bytes 2433024 | tf_op jit(solution)/shard_map/reduce_scatter | solution.py:305
  3907.4 4.7 copy-start.40
  3915.0 400.9 %reduce-scatter.17.cloned.1.call-start = ((), (), s32[]{:S(2)}) async-start(), calls=%async_computation.11 | async-start | bytes 9732096 | tf_op jit(solution)/shard_map/reduce_scatter | solution.py:309
  3928.1 529.9 %reduce-scatter.15.cloned.1.call-start = ((), (), s32[]{:S(2)}) async-start(), calls=%async_computation.10 | async-start | bytes 9732096 | tf_op jit(solution)/shard_map/reduce_scatter | solution.py:308
  3939.4 3.4 copy-start.29
  3942.8 12.8 copy-start.35
  3942.8 12.8 copy-start.65
  3957.1 4.0 copy-start.61
  3957.2 45.0 %copy-start.55 = (f32[1,4,2,128]{3,1,2,0:T(4,128)S(1)}, f32[1,4,2,128]{3,1,2,0:T(4,128)}, u32[]{:S(2)}) copy-start(f32[1,4,2,128]{3,1,2,0:T(4,128)} %copy-done.54) | copy-start | bytes 12292
  (23 other events, 36.4 us)
Sparse Core Ops, SparseCore 0:
  909.4 355.2 reduce-scatter.12
  3440.5 525.8 reduce-scatter.6
  3972.2 97.9 reduce-scatter.8
  4076.8 98.0 reduce-scatter.10
  4181.3 134.5 reduce-scatter.16
  4323.2 134.6 reduce-scatter.14
where the time goes:
time: 4480 us; the launch traced here: 4460 us
  starting transfers between devices  1820 us (41%)
  waiting for transfers between devices  1310 us (29%)
  matrix products  910 us (20%)
  other arithmetic  124 us (3%)
  loops' own time  122 us (3%)
  local copies, waits for them, and re-layouts  116 us (3%)
    ppermute x7, starting transfers between devices, from_behind_2(): return lax.ppermute(x, axis, [(i, (i + by) % size) for i in range(size)])  944 us
    ppermute x9, starting transfers between devices, from_behind(): return lax.ppermute(block, axis, route)  879 us
    ppermute x7, waiting for transfers between devices, from_behind_2(): return lax.ppermute(x, axis, [(i, (i + by) % size) for i in range(size)])  859 us
    dot_general x4, matrix products, block_scores(): jnp.einsum('rhqk,hg->rgqk', scaled, mix_pre, precision=PRECISE)  292 us
    reduce_scatter x1, waiting for transfers between devices, shards(): lax.psum_scatter(grad_ff_in, ('dp', 'blk'), scatter_dimension=0, tiled=True)  142 us
    reduce_scatter x1, waiting for transfers between devices, shards(): lax.psum_scatter(grad_ff_out, ('dp', 'blk'), scatter_dimension=0, tiled=T...  141 us
    dot_general x18, matrix products, matmul(): return jnp.dot(former, latter, preferred_element_type=jnp.float32)  106 us
    reduce_scatter x1, waiting for transfers between devices, shards(): lax.psum_scatter(grad_value, ('dp', 'blk'), scatter_dimension=0, tiled=True)  105 us
  transfers between devices with their start and end apart: 22, of which 15 were waited for; matrix products, arithmetic and copies ran while one was open for 23% of the time, Pallas kernels for 0%

commit v1 on v0

v1 whole, which is shorter than its diff:
```python
import functools

import jax
import jax.numpy as jnp
from jax import lax
from jax.experimental import pallas as pl
from jax.experimental.pallas import tpu as pltpu
from jax.sharding import PartitionSpec as P

F32 = jnp.float32
BF16 = jnp.bfloat16
EPSILON = 1e-06
MASKED = -1e30
PER = 6


def dot(a, b):
    return jnp.dot(a, b, preferred_element_type=F32)


def fwd_kernel(tile, heads, per, tasks_row, info, place, pre, post, q_ref, k_ref, v_ref,
               att_ref, u_ref, inv_ref, p_out, qa, vt, s_all, u_acc, att_acc, top, mass, p_buf, sems):
    task, part = pl.program_id(0), pl.program_id(1)
    parts = heads // per
    width = q_ref.shape[2]
    size = width // heads
    first, count = info[task, 0], info[task, 1]
    row_len = k_ref.shape[1]

    @pl.when((task % tasks_row == 0) & (part == 0))
    def _():
        for c in range(row_len // tile):
            vt[:, c * tile:(c + 1) * tile] = v_ref[0, c * tile:(c + 1) * tile, :].T

    qt = q_ref[0].astype(F32).T
    for g in range(per):
        for h in range(heads):
            rows = slice(h * size, (h + 1) * size)
            qa[rows, g * tile:(g + 1) * tile] = (qt[rows] * (pre[h, part * per + g] * size ** -0.5)).astype(BF16)

    def cols(g):
        return slice(g * tile, (g + 1) * tile)

    def keys(j):
        return pl.ds(pl.multiple_of(place[first + j] * tile, tile), tile)

    last = count - 1
    causal = lax.broadcasted_iota(jnp.int32, (tile, tile), 0) <= lax.broadcasted_iota(jnp.int32, (tile, tile), 1)
    kj = k_ref[0, keys(last), :]
    for g in range(per):
        s = jnp.where(causal, dot(kj, qa[:, cols(g)]), MASKED)
        s_all[last, :, cols(g)] = s
        top[:, cols(g)] = jnp.max(s, axis=0, keepdims=True)

    def scores(j, carry):
        kj = k_ref[0, keys(j), :]
        for g in range(per):
            s = dot(kj, qa[:, cols(g)])
            s_all[j, :, cols(g)] = s
            top[:, cols(g)] = jnp.maximum(top[:, cols(g)], jnp.max(s, axis=0, keepdims=True))
        return carry

    lax.fori_loop(0, last, scores, 0)
    u_acc[...] = jnp.zeros_like(u_acc)
    mass[...] = jnp.zeros_like(mass)

    def copy(j, slot):
        return pltpu.make_async_copy(p_buf.at[slot], p_out.at[task, part, j], sems.at[slot])

    def sums(j, carry):
        slot = j % 2

        @pl.when(j >= 2)
        def _():
            copy(j, slot).wait()
        vj = vt[:, keys(j)]
        for g in range(per):
            p = jnp.exp(s_all[j, :, cols(g)] - top[:, cols(g)])
            mass[:, cols(g)] += jnp.sum(p, axis=0, keepdims=True)
            low = p.astype(BF16)
            p_buf[slot, :, cols(g)] = low
            u_acc[:, cols(g)] += dot(vj, low)
        copy(j, slot).start()
        return carry

    lax.fori_loop(0, count, sums, 0)

    inv = 1.0 / mass[...]
    inv_ref[0, 0] = inv
    u_ref[0, 0] = u_acc[...].astype(BF16)
    for h in range(heads):
        rows = slice(h * size, (h + 1) * size)
        acc = None
        for g in range(per):
            term = u_acc[rows, cols(g)] * (inv[:, cols(g)] * post[part * per + g, h])
            acc = term if acc is None else acc + term
        att_acc[rows] = jnp.where(part == 0, acc, acc + att_acc[rows])

    @pl.when(part == parts - 1)
    def _():
        att_ref[0] = att_acc[...].T.astype(BF16)

    @pl.when(count >= 2)
    def _():
        copy(0, count % 2).wait()
    copy(0, (count - 1) % 2).wait()


def fwd(info, place, pre, post, q, k, v, tile, per):
    tasks, _, width = q.shape
    rows, row_len, _ = k.shape
    heads = pre.shape[0]
    parts = heads // per
    tiles = row_len // tile
    wide = per * tile
    tasks_row = tasks // rows
    smem = pl.BlockSpec(memory_space=pltpu.SMEM)
    return pl.pallas_call(
        functools.partial(fwd_kernel, tile, heads, per, tasks_row),
        grid=(tasks, parts),
        in_specs=[
            smem, smem, smem, smem,
            pl.BlockSpec((1, tile, width), lambda t, p: (t, 0, 0)),
            pl.BlockSpec((1, row_len, width), lambda t, p: (t // tasks_row, 0, 0)),
            pl.BlockSpec((1, row_len, width), lambda t, p: (t // tasks_row, 0, 0)),
        ],
        out_specs=[
            pl.BlockSpec((1, tile, width), lambda t, p: (t, 0, 0)),
            pl.BlockSpec((1, 1, width, wide), lambda t, p: (t, p, 0, 0)),
            pl.BlockSpec((1, 1, 1, wide), lambda t, p: (t, p, 0, 0)),
            pl.BlockSpec(memory_space=pl.ANY),
        ],
        out_shape=[
            jax.ShapeDtypeStruct((tasks, tile, width), BF16),
            jax.ShapeDtypeStruct((tasks, parts, width, wide), BF16),
            jax.ShapeDtypeStruct((tasks, parts, 1, wide), F32),
            jax.ShapeDtypeStruct((tasks, parts, tiles, tile, wide), BF16),
        ],
        scratch_shapes=[
            pltpu.VMEM((width, wide), BF16),
            pltpu.VMEM((width, row_len), BF16),
            pltpu.VMEM((tiles, tile, wide), F32),
            pltpu.VMEM((width, wide), F32),
            pltpu.VMEM((width, tile), F32),
            pltpu.VMEM((1, wide), F32),
            pltpu.VMEM((1, wide), F32),
            pltpu.VMEM((2, tile, wide), BF16),
            pltpu.SemaphoreType.DMA((2,)),
        ],
        compiler_params=pltpu.CompilerParams(vmem_limit_bytes=60 * 2 ** 20),
        name="attention_forward",
    )(info, place, pre, post, q, k, v)


def bwd_kernel(tile, heads, per, tasks_row, info, place, pre, post, q_ref, da_ref, k_ref, v_ref, u_ref, inv_ref, pre_wide, post_wide, p_in,
               dq_ref, dk_ref, dv_ref, gpre_ref, gpost_ref,
               kt, qb, daa, dab, w_acc, dq_acc, dk_acc, dv_acc, delta, dm_all, p_buf, sems):
    task, part = pl.program_id(0), pl.program_id(1)
    parts = heads // per
    width = q_ref.shape[2]
    size = width // heads
    first, count = info[task, 0], info[task, 1]
    row_len = k_ref.shape[1]

    def cols(g):
        return slice(g * tile, (g + 1) * tile)

    def keys(j):
        return pl.ds(pl.multiple_of(place[first + j] * tile, tile), tile)

    def copy(j, slot):
        return pltpu.make_async_copy(p_in.at[task, part, j], p_buf.at[slot], sems.at[slot])

    copy(0, 0).start()

    @pl.when((task % tasks_row == 0) & (part == 0))
    def _():
        for c in range(row_len // tile):
            kt[:, c * tile:(c + 1) * tile] = k_ref[0, c * tile:(c + 1) * tile, :].T
        dk_acc[...] = jnp.zeros_like(dk_acc)
        dv_acc[...] = jnp.zeros_like(dv_acc)

    @pl.when((task == 0) & (part == 0))
    def _():
        gpre_ref[...] = jnp.zeros_like(gpre_ref)
        gpost_ref[...] = jnp.zeros_like(gpost_ref)

    w_acc[...] = jnp.zeros_like(w_acc)
    qf = q_ref[0].astype(F32)
    daf = da_ref[0].astype(F32)
    qt = qf.T
    dat = daf.T
    inv = inv_ref[0, 0]
    for g in range(per):
        qb[cols(g), :] = (qf * pre_wide[0, g:g + 1, :]).astype(BF16)
        inv_g = inv[:, cols(g)]
        d_g = None
        for h in range(heads):
            rows = slice(h * size, (h + 1) * size)
            scaled = dat[rows] * inv_g
            weight = post[part * per + g, h]
            daa[rows, cols(g)] = (scaled * weight).astype(BF16)
            e = jnp.sum(scaled * u_ref[0, 0, rows, cols(g)].astype(F32), axis=0, keepdims=True)
            gpost_ref[part, g, h:h + 1, :] += e
            d_g = e * weight if d_g is None else d_g + e * weight
        delta[:, cols(g)] = d_g * inv_g
        dab[cols(g), :] = daa[:, cols(g)].astype(F32).T.astype(BF16)

    def step(j, carry):
        slot = j % 2
        copy(j, slot).wait()

        @pl.when(j + 1 < count)
        def _():
            copy(j + 1, 1 - slot).start()
        vj = v_ref[0, keys(j), :]
        ktj = kt[:, keys(j)]
        for g in range(per):
            dp = dot(vj, daa[:, cols(g)])
            dm = (p_buf[slot, :, cols(g)].astype(F32) * (dp - delta[:, cols(g)])).astype(BF16)
            dm_all[:, cols(g)] = dm
            w_acc[:, cols(g)] += dot(ktj, dm)
        dv_acc[keys(j), :] += dot(p_buf[slot], dab[...])
        dk_acc[keys(j), :] += dot(dm_all[...], qb[...])
        return carry

    lax.fori_loop(0, count, step, 0)

    for h in range(heads):
        rows = slice(h * size, (h + 1) * size)
        acc = None
        for g in range(per):
            w = w_acc[rows, cols(g)]
            term = w * (pre[h, part * per + g] * size ** -0.5)
            acc = term if acc is None else acc + term
            gpre_ref[part, g, h:h + 1, :] += jnp.sum(w * qt[rows], axis=0, keepdims=True) * size ** -0.5
        dq_acc[rows] = jnp.where(part == 0, acc, acc + dq_acc[rows])

    @pl.when(part == parts - 1)
    def _():
        dq_ref[0] = dq_acc[...].T.astype(BF16)

    @pl.when((task % tasks_row == tasks_row - 1) & (part == parts - 1))
    def _():
        dk_ref[0] = dk_acc[...].astype(BF16)
        dv_ref[0] = dv_acc[...].astype(BF16)


def bwd(info, place, pre, post, q, da, k, v, u, inv, p, tile, per):
    tasks, _, width = q.shape
    rows, row_len, _ = k.shape
    heads = pre.shape[0]
    parts = heads // per
    tiles = row_len // tile
    wide = per * tile
    tasks_row = tasks // rows
    size = width // heads
    pre_wide = jnp.repeat(pre.T * size ** -0.5, size, axis=1).reshape(parts, per, width)
    post_wide = jnp.repeat(post, size, axis=1).reshape(parts, per, width)
    smem = pl.BlockSpec(memory_space=pltpu.SMEM)
    once = pl.Buffered(1)
    row_spec = pl.BlockSpec((1, row_len, width), lambda t, p: (t // tasks_row, 0, 0))
    out = pl.pallas_call(
        functools.partial(bwd_kernel, tile, heads, per, tasks_row),
        grid=(tasks, parts),
        in_specs=[
            smem, smem, smem, smem,
            pl.BlockSpec((1, tile, width), lambda t, p: (t, 0, 0)),
            pl.BlockSpec((1, tile, width), lambda t, p: (t, 0, 0)),
            pl.BlockSpec((1, row_len, width), lambda t, p: (t // tasks_row, 0, 0), pipeline_mode=once),
            pl.BlockSpec((1, row_len, width), lambda t, p: (t // tasks_row, 0, 0), pipeline_mode=once),
            pl.BlockSpec((1, 1, width, wide), lambda t, p: (t, p, 0, 0)),
            pl.BlockSpec((1, 1, 1, wide), lambda t, p: (t, p, 0, 0)),
            pl.BlockSpec((1, per, width), lambda t, p: (p, 0, 0)),
            pl.BlockSpec((1, per, width), lambda t, p: (p, 0, 0)),
            pl.BlockSpec(memory_space=pl.ANY),
        ],
        out_specs=[
            pl.BlockSpec((1, tile, width), lambda t, p: (t, 0, 0)),
            row_spec, row_spec,
            pl.BlockSpec((parts, per, heads, tile), lambda t, p: (0, 0, 0, 0)),
            pl.BlockSpec((parts, per, heads, tile), lambda t, p: (0, 0, 0, 0)),
        ],
        out_shape=[
            jax.ShapeDtypeStruct((tasks, tile, width), BF16),
            jax.ShapeDtypeStruct((rows, row_len, width), BF16),
            jax.ShapeDtypeStruct((rows, row_len, width), BF16),
            jax.ShapeDtypeStruct((parts, per, heads, tile), F32),
            jax.ShapeDtypeStruct((parts, per, heads, tile), F32),
        ],
        scratch_shapes=[
            pltpu.VMEM((width, row_len), BF16),
            pltpu.VMEM((wide, width), BF16),
            pltpu.VMEM((width, wide), BF16),
            pltpu.VMEM((wide, width), BF16),
            pltpu.VMEM((width, wide), F32),
            pltpu.VMEM((width, tile), F32),
            pltpu.VMEM((row_len, width), F32),
            pltpu.VMEM((row_len, width), F32),
            pltpu.VMEM((1, wide), F32),
            pltpu.VMEM((tile, wide), BF16),
            pltpu.VMEM((2, tile, wide), BF16),
            pltpu.SemaphoreType.DMA((2,)),
        ],
        compiler_params=pltpu.CompilerParams(vmem_limit_bytes=62 * 2 ** 20),
        name="attention_backward",
    )(info, place, pre, post, q, da, k, v, u, inv, pre_wide, post_wide, p)
    dq, dk, dv, gpre, gpost = out
    return dq, dk, dv, jnp.sum(gpre, axis=3).reshape(heads, heads).T, jnp.sum(gpost, axis=3).reshape(heads, heads)


def inverse_rms(values):
    return lax.rsqrt(jnp.mean(values * values, axis=-1, keepdims=True) + EPSILON)


def transposed_dot(a, b):
    return lax.dot_general(a, b, (((0,), (0,)), ((), ())), preferred_element_type=F32)


def dot_transposed(a, b):
    return lax.dot_general(a, b, (((1,), (1,)), ((), ())), preferred_element_type=F32)


def swap(value, axis, bit):
    return lax.ppermute(value, axis, [(i, i ^ bit) for i in range(lax.axis_size(axis))])


def bits_down(size):
    bit = size // 2
    while bit:
        yield bit
        bit //= 2


def gather_blocks(block, axis):
    masks, held = [0], block[None]
    for bit in bits_down(lax.axis_size(axis)):
        held = jnp.concatenate((held, swap(held, axis, bit)), axis=0)
        masks = masks + [m ^ bit for m in masks]
    return held, masks


def scatter_blocks(parts, masks, axis):
    held = {m: parts[i] for i, m in enumerate(masks)}
    for bit in reversed(list(bits_down(lax.axis_size(axis)))):
        away = sorted(m for m in held if m & bit)
        sent = jnp.stack([held[m].astype(BF16) for m in away])
        came = swap(sent, axis, bit)
        held = {m: v for m, v in held.items() if not m & bit}
        for i, m in enumerate(away):
            held[m ^ bit] = held[m ^ bit].astype(F32) + came[i].astype(F32)
    return held[0]


def scatter_grad(grad):
    groups, circle = lax.axis_size("dp"), lax.axis_size("blk")
    rows = grad.shape[0] // (groups * circle)
    held = grad.reshape(groups, circle, rows, -1)
    own = lax.axis_index("blk")
    bit = 1
    while bit < circle:
        halves = held.reshape(groups, circle // (2 * bit), 2, rows, -1)
        side = (own // bit) % 2
        kept = lax.dynamic_index_in_dim(halves, side, 2, keepdims=False)
        sent = lax.dynamic_index_in_dim(halves, 1 - side, 2, keepdims=False).astype(BF16)
        held = kept.astype(F32) + swap(sent, "blk", bit).astype(F32)
        bit *= 2
    held = held.reshape(groups, rows, -1)
    mine = lax.axis_index("dp")
    total = lax.dynamic_index_in_dim(held, mine, 0, keepdims=False)
    for step in range(1, groups):
        sent = lax.dynamic_index_in_dim(held, mine ^ step, 0, keepdims=False).astype(BF16)
        total = total + swap(sent, "dp", step).astype(F32)
    return total.reshape((rows,) + grad.shape[1:])


class Plan:
    def __init__(self, rows, span, circle):
        self.tile = min(256, span)
        self.rows, self.circle = rows, circle
        self.slots = span // self.tile
        self.tiles = self.slots * circle
        self.groups = {}
        for r in range(rows):
            for c in range(self.slots):
                route = tuple((b, self.worker(r, b * self.slots + c)) for b in range(circle))
                self.groups.setdefault(route, []).append((r, c))

    def worker(self, r, tile):
        lap, place = divmod(tile, self.circle)
        return place if (lap + r * (self.slots % 2)) % 2 == 0 else self.circle - 1 - place

    def table(self):
        found = [[[0] * self.circle for _ in range(self.slots)] for _ in range(self.rows)]
        for route, places in self.groups.items():
            for r, c in places:
                for b, d in route:
                    found[r][c][d] = b * self.slots + c
        return found

    def move(self, block, back=False):
        shape = block.shape
        cut = block.reshape((self.rows * self.slots, self.tile) + shape[2:])
        out = [None] * (self.rows * self.slots)
        for route, places in self.groups.items():
            at = [r * self.slots + c for r, c in places]
            piece = cut[jnp.array(at)] if len(at) < cut.shape[0] else cut
            pairs = [(d, b) for b, d in route] if back else list(route)
            if any(b != d for b, d in pairs):
                piece = lax.ppermute(piece, "blk", pairs)
            for i, a in enumerate(at):
                out[a] = piece[i]
        return jnp.stack(out)


def shards(
    inputs,
    doc_lengths,
    norm1_gain,
    w_query,
    w_key,
    w_value,
    head_mix_pre,
    head_mix_post,
    w_attn_out,
    norm2_gain,
    w_ff_in,
    w_ff_out,
    out_cotangent,
):
    rows, span, width = inputs.shape
    circle = lax.axis_size("blk")
    own = lax.axis_index("blk")
    plan = Plan(rows, span, circle)
    tile, slots, tiles = plan.tile, plan.slots, plan.tiles
    tasks = rows * slots
    row_len = span * circle

    gathered, masks = gather_blocks(inputs, "blk")
    cotangent = plan.move(out_cotangent).reshape(tasks * tile, width)

    place_of = [0] * circle
    for p, m in enumerate(masks):
        place_of[m] = p
    place_of = jnp.array(place_of, jnp.int32)
    key_place = place_of[jnp.arange(tiles, dtype=jnp.int32) // slots ^ own] * slots + jnp.arange(tiles, dtype=jnp.int32) % slots
    work = jnp.array(plan.table(), jnp.int32)[:, :, own]
    bounds = jnp.cumsum(doc_lengths, axis=1)
    begin = jnp.max(jnp.where(bounds[:, None, :] <= work[:, :, None] * tile, bounds[:, None, :], 0), axis=2) // tile
    info = jnp.stack((begin, work - begin + 1), axis=2).reshape(tasks, 2).astype(jnp.int32)
    places = key_place[work]

    x_all = gathered.transpose(1, 0, 2, 3).reshape(rows * row_len, width).astype(F32)
    scale_all = inverse_rms(x_all)
    normed_all = (x_all * scale_all * norm1_gain).astype(BF16)
    keys = jnp.dot(normed_all, w_key, preferred_element_type=F32).astype(BF16).reshape(rows, row_len, width)
    values = jnp.dot(normed_all, w_value, preferred_element_type=F32).astype(BF16).reshape(rows, row_len, width)

    def of_tasks(array):
        cut = array.reshape(rows, tiles, tile, width)
        picked = [lax.dynamic_index_in_dim(cut[r], places[r, c], 0, keepdims=False) for r in range(rows) for c in range(slots)]
        return jnp.concatenate(picked, axis=0)

    normed_own = of_tasks(normed_all)
    x_own = of_tasks(gathered.transpose(1, 0, 2, 3)).astype(F32)
    queries = jnp.dot(normed_own, w_query, preferred_element_type=F32).astype(BF16).reshape(tasks, tile, width)

    attended, sums, inverse, probs = fwd(info, key_place, head_mix_pre, head_mix_post, queries, keys, values, tile, PER)
    attended = attended.reshape(tasks * tile, width)

    middle = x_own + jnp.dot(attended, w_attn_out, preferred_element_type=F32)
    scale_two = inverse_rms(middle)
    normed_two = (middle * scale_two * norm2_gain).astype(BF16)
    hidden = jnp.dot(normed_two, w_ff_in, preferred_element_type=F32)
    active, pull_gelu = jax.vjp(jax.nn.gelu, hidden)
    active = active.astype(BF16)
    output = (middle + jnp.dot(active, w_ff_out, preferred_element_type=F32)).astype(BF16)
    output = plan.move(output.reshape(rows, span, width), back=True).reshape(rows, span, width)
    grad_ff_out = transposed_dot(active, cotangent)
    d_hidden = pull_gelu(dot_transposed(cotangent, w_ff_out))[0].astype(BF16)
    grad_ff_in = transposed_dot(normed_two, d_hidden)
    d_normed_two = dot_transposed(d_hidden, w_ff_in)
    grad_gain_two = jnp.sum(d_normed_two * middle * scale_two, axis=0)
    z = norm2_gain * d_normed_two
    d_middle = cotangent.astype(F32) + scale_two * z - middle * scale_two ** 3 * jnp.mean(z * middle, axis=1, keepdims=True)
    d_branch = d_middle.astype(BF16)
    grad_attn_out = transposed_dot(attended, d_branch)
    d_attended = dot_transposed(d_branch, w_attn_out).astype(BF16).reshape(tasks, tile, width)

    d_queries, d_keys, d_values, grad_pre, grad_post = bwd(
        info, key_place, head_mix_pre, head_mix_post, queries, d_attended, keys, values, sums, inverse, probs, tile, PER
    )
    d_queries = d_queries.reshape(tasks * tile, width)
    d_keys = d_keys.reshape(rows * row_len, width)
    d_values = d_values.reshape(rows * row_len, width)
    grad_query = transposed_dot(normed_own, d_queries)
    grad_key = transposed_dot(normed_all, d_keys)
    grad_value = transposed_dot(normed_all, d_values)

    def norm_one_back(d_normed, x):
        scale = inverse_rms(x)
        y = norm1_gain * d_normed
        gain = jnp.sum(d_normed * x * scale, axis=0)
        return scale * y - x * scale ** 3 * jnp.mean(y * x, axis=1, keepdims=True), gain

    d_all, gain_all = norm_one_back(dot_transposed(d_keys, w_key) + dot_transposed(d_values, w_value), x_all)
    d_own, gain_own = norm_one_back(dot_transposed(d_queries, w_query), x_own)
    d_own = (d_own + d_middle).reshape(tasks, tile, width)
    d_all = d_all.reshape(rows, tiles, tile, width)
    for r in range(rows):
        for c in range(slots):
            at = (r, places[r, c], 0, 0)
            d_all = lax.dynamic_update_slice(d_all, lax.dynamic_slice(d_all, at, (1, 1, tile, width)) + d_own[r * slots + c][None, None], at)
    d_all = d_all.reshape(rows, circle, span, width).transpose(1, 0, 2, 3)
    input_grad = scatter_blocks(d_all, masks, "blk").astype(BF16)

    small = lax.psum((gain_all + gain_own, grad_gain_two, grad_pre, grad_post), ("dp", "blk"))
    index = lax.axis_index("dp") * circle + own
    share = width // (lax.axis_size("dp") * circle)

    def part(gain):
        return lax.dynamic_slice_in_dim(gain, index * share, share)

    return (
        output,
        input_grad,
        part(small[0]),
        scatter_grad(grad_query),
        scatter_grad(grad_key),
        scatter_grad(grad_value),
        small[2],
        small[3],
        scatter_grad(grad_attn_out),
        part(small[1]),
        scatter_grad(grad_ff_in),
        scatter_grad(grad_ff_out),
    )


def solution(mesh):
    tokens = P("dp", "blk", None)
    split = P(("dp", "blk"), None)
    in_specs = (tokens, P("dp", None)) + (P(),) * 10 + (tokens,)
    out_specs = (tokens, tokens, P(("dp", "blk")), split, split, split, P(), P(), split, P(("dp", "blk")), split, split)
    return jax.shard_map(shards, mesh=mesh, in_specs=in_specs, out_specs=out_specs, check_vma=False)
```

time: 4480 us -> 788 us (0.18)
  starting transfers between devices: 1820 us -> 137 us
  waiting for transfers between devices: 1310 us -> 102 us
  matrix products: 910 us -> 130 us
  Pallas kernels: 0 us -> 166 us
  loops' own time: 122 us -> 0 us
  other arithmetic: 124 us -> 67.9 us
    ppermute x16 -> x62, starting transfers between devices: 1820 us -> 137 us  [the longest x58 99.8 us: swap(): lax.ppermute(value, axis, [(i, i ^ bit) for i in range(lax.axis_size(axis...]
    dot_general x39 -> x18, matrix products: 910 us -> 130 us  [the longest x6 56.7 us: dot_transposed(): lax.dot_general(a, b, (((1,), (1,)), ((), ())), preferred_element_type=F32)]
    ppermute x16 -> x62, waiting for transfers between devices: 863 us -> 102 us  [the longest x58 102 us: swap(): lax.ppermute(value, axis, [(i, i ^ bit) for i in range(lax.axis_size(axis...]
    reduce_scatter x6 -> x0, waiting for transfers between devices: 451 us -> none  [the longest x1 142 us: shards(): lax.psum_scatter(grad_ff_in, ('dp', 'blk'), scatter_dimension=0, tiled=True)]
    pallas_call x0 -> x2, Pallas kernels: none -> 166 us  [the longest x1 111 us: bwd(): pl.pallas_call(functools.partial(bwd_kernel, tile, heads, per, tasks_row)...]
    another operation x20 -> x0, loops' own time: 122 us -> none  [the longest x3 44 us: travel(): current, status = lax.fori_loop(0, turns - 1, advance, (moving, totals))]
    psum x0 -> x1, blocking collectives: none -> 77.5 us  [shards(): lax.psum((gain_all + gain_own, grad_gain_two, grad_pre, grad_post), ('dp'...]
  transfers between devices with their start and end apart: 22 -> 62, of which waited for: 15 -> 19; matrix products, arithmetic and copies ran while one was open for 23% -> 20% of each run, Pallas kernels for 0% -> 14%
where the time goes in v1:
time: 788 us; the launch traced here: 779 us
  Pallas kernels  166 us (21%)
  starting transfers between devices  137 us (17%)
  matrix products  130 us (16%)
  waiting for transfers between devices  102 us (13%)
  local copies, waits for them, and re-layouts  88.1 us (11%)
  blocking collectives  77.5 us (10%)
  other arithmetic  67.9 us (9%)
  between operations  10.2 us (1%)
    pallas_call x1, Pallas kernels, bwd(): pl.pallas_call(functools.partial(bwd_kernel, tile, heads, per, tasks_row)...  111 us
    ppermute x58, waiting for transfers between devices, swap(): lax.ppermute(value, axis, [(i, i ^ bit) for i in range(lax.axis_size(axis...  102 us
    ppermute x58, starting transfers between devices, swap(): lax.ppermute(value, axis, [(i, i ^ bit) for i in range(lax.axis_size(axis...  99.8 us
    psum x1, blocking collectives, shards(): lax.psum((gain_all + gain_own, grad_gain_two, grad_pre, grad_post), ('dp'...  77.5 us
    dot_general x6, matrix products, dot_transposed(): lax.dot_general(a, b, (((1,), (1,)), ((), ())), preferred_element_type=F32)  56.7 us
    pallas_call x1, Pallas kernels, fwd(): pl.pallas_call(functools.partial(fwd_kernel, tile, heads, per, tasks_row)...  54.6 us
    ppermute x4, starting transfers between devices, move(): piece = lax.ppermute(piece, 'blk', pairs)  37.5 us
    dot_general x6, matrix products, transposed_dot(): lax.dot_general(a, b, (((0,), (0,)), ((), ())), preferred_element_type=F32)  33.7 us
  transfers between devices with their start and end apart: 62, of which 19 were waited for; matrix products, arithmetic and copies ran while one was open for 20% of the time, Pallas kernels for 14%

profile of v1, /device:TPU:0, one launch (start us, length us, event | category | flops | bytes accessed | tf_op | source)
XLA Modules:
  0.0 779.4 jit_solution(5153005379837975139)
XLA Ops:
  0.7 3.0 collective-permute-start
  3.7 34.6 %collective-permute-done = bf16[1,2,512,768]{3,2,1,0:T(8,128)(2,1)S(1)} collective-permute-done((bf16[1,2,512,768]{3,2,1,0:T(8,128)(2,1)}, bf16[1,2,512,768]{3,2,1,0:T(8,128)(2,1)S(1)}, u32[]{:S(2)}, u32[]{:S(2)}) %collective-permute-start) | collective-permute-done | bytes 1572896 | tf_op jit(solution)/shard_map/ppermute | solution.py:325
  38.3 3.4 pad_maximum_fusion
  43.3 7.4 collective-permute-start.4
  70.9 3.7 multiply_reduce_fusion
  74.6 2.6 copy-done.6
  79.3 3.9 copy.107
  88.0 3.0 fusion.152
  91.0 6.9 convolution_convert_fusion
  97.9 6.9 convolution_convert_fusion.1
  108.0 2.5 convolution_convert_fusion.3
  111.5 54.6 %attention_forward.1 = (bf16[4,256,768]{2,1,0:T(8,128)(2,1)}, bf16[4,2,768,1536]{3,2,1,0:T(8,128)(2,1)}, f32[4,2,1,1536]{3,2,1,0:T(1,128)}, bf16[4,2,8,256,1536]{4,3,2,1,0:T(8,128)(2,1)}) custom-call(s32[4,2]{1,0:T(4,128)} %pad_add_fusion.info, s32[8]{0:T(128)} %copy-done.2, f32[12,12]{1,0:T(8,128)} %pre.3, f32[12,12]{1,0:T(8,128)} %post.3, ...), custom_call_target="tpu_custom_call" | custom-call | tf_op jit(solution)/shard_map/attention_forward/pallas_call | solution.py:118
  166.1 3.4 multiply_reduce_fusion.3
  169.6 11.6 %fusion.14 = (bf16[3072,1024]{0,1:T(8,128)(2,1)}, f32[1024,3072]{1,0:T(8,128)S(1)}) fusion(bf16[768,3072]{1,0:T(8,128)(2,1)} %param.29, f32[1024,768]{1,0:T(8,128)S(1)} %get-tuple-element.175, f32[768]{0:T(1024)S(1)} %copy-done.46, f32[1024]{0:T(1024)S(1)} %get-tuple-element.167), kind=kOutput, calls=%fused_computation.23 | convolution fusion | flops 4862509056 | bytes 26745856 | tf_op jit(solution)/shard_map/dot_general | solution.py:474
  181.2 8.6 %add_convert_fusion = bf16[1024,768]{1,0:T(8,128)(2,1)} fusion(f32[1024,768]{1,0:T(8,128)S(1)} %get-tuple-element.175, bf16[3072,768]{1,0:T(8,128)(2,1)S(1)} %bitcast.426, f32[1024,3072]{1,0:T(8,128)S(1)} %get-tuple-element.180), kind=kOutput, calls=%fused_computation.69 | convolution fusion | flops 4861722624 | bytes 22020096 | tf_op jit(solution)/shard_map/dot_general | solution.py:477
  189.8 3.2 gather_fusion.3
  193.0 3.1 gather_fusion.2
  196.1 14.2 %fusion.6 = bf16[1024,3072]{1,0:T(8,128)(2,1)S(1)} fusion(f32[1024,3072]{1,0:T(8,128)} %copy-done.57, bf16[1024,768]{1,0:T(8,128)(2,1)S(1)} %bitcast.396, bf16[3072,768]{1,0:T(8,128)(2,1)} %param.30), kind=kOutput, calls=%fused_computation.15 | convolution fusion | flops 4894752768 | bytes 25165824 | tf_op jit(solution)/shard_map/dot_general | solution.py:321
  210.3 9.9 %multiply_reduce_fusion.1 = (f32[768]{0:T(1024)}, f32[1024]{0:T(1024)}, f32[1024,768]{1,0:T(8,128)}) fusion(f32[1024,768]{1,0:T(8,128)S(1)} %copy-done.21, f32[1024]{0:T(1024)S(1)} %get-tuple-element.167, f32[768]{0:T(1024)S(1)} %copy-done.46, bf16[1024,3072]{1,0:T(8,128)(2,1)S(1)} %fusion.6, bf16[768,3072]{1,0:T(8,128)(2,1)} %param.29), kind=kOutput, calls=%fused_computation.66 | convolution fusion | flops 4836554752 | bytes 17315840 | tf_op jit(solution)/shard_map/dot_general | solution.py:321
  220.2 7.9 %fusion.149 = f32[768,3072]{1,0:T(8,128)} fusion(bf16[1024,3072]{1,0:T(8,128)(2,1)S(1)} %fusion.6, f32[1024,768]{1,0:T(8,128)S(1)} %copy-done.21, f32[768]{0:T(1024)S(1)} %copy-done.46, f32[1024]{0:T(1024)S(1)} %get-tuple-element.167), kind=kOutput, calls=%fused_computation.309 | convolution fusion | flops 4834197504 | bytes 18881536 | tf_op jit(solution)/shard_map/dot_general | solution.py:317
  228.2 8.8 %copy.112 = bf16[768,4096]{1,0:T(8,128)(2,1)} copy(bf16[768,4096]{0,1:T(8,128)(2,1)} %bitcast.379) | data formatting | bytes 12582912 | tf_op jit(solution)/shard_map/dot_general | solution.py:317
  241.0 8.7 %copy.115 = bf16[3072,1024]{1,0:T(8,128)(2,1)} copy(bf16[3072,1024]{0,1:T(8,128)(2,1)} %get-tuple-element.179) | data formatting | bytes 12582912 | tf_op jit(solution)/shard_map/convert_element_type | solution.py:476
  249.7 7.4 collective-permute-start.2
  257.1 20.8 %collective-permute-start.3 = (bf16[2,256,768]{2,1,0:T(8,128)(2,1)}, bf16[2,256,768]{2,1,0:T(8,128)(2,1)}, u32[]{:S(2)}, u32[]{:S(2)}) collective-permute-start(bf16[2,256,768]{2,1,0:T(8,128)(2,1)} %gather_fusion.3), channel_id=1, source_target_pairs={{1,0},{3,1},{2,2},{0,3},{5,4},{7,5},{6,6},{4,7},{9,8},{11,9},{10,1... | collective-permute-start | bytes 2359304 | tf_op jit(solution)/shard_map/ppermute | solution.py:410
  278.6 3.8 multiply_subtract_fusion
  282.4 2.6 convolution_convert_fusion.2
  288.0 111.0 %attention_backward.1 = (bf16[4,256,768]{2,1,0:T(8,128)(2,1)}, bf16[2,2048,768]{2,1,0:T(8,128)(2,1)}, bf16[2,2048,768]{2,1,0:T(8,128)(2,1)}, f32[2,6,12,256]{3,2,1,0:T(8,128)}, f32[2,6,12,256]{3,2,1,0:T(8,128)}) custom-call(s32[4,2]{1,0:T(4,128)} %pad_add_fusion.info, s32[8]{0:T(128)} %copy-done.2, f32[12,12]{1,0:T(8,128)} %pre.3, f32[12,12]{1,0:T(8,128)} %post.3, ...), custom_call_target="tpu_custom_call" | custom-call | tf_op jit(solution)/shard_map/attention_backward/pallas_call | solution.py:263
  399.1 2.9 fusion.159
  402.9 5.9 collective-permute-start.8
  408.9 7.6 fusion.161
  416.6 6.7 fusion.160
  425.5 5.0 fusion.29
  430.5 8.3 %fusion.158 = f32[4096,768]{1,0:T(8,128)} fusion(bf16[4096,768]{1,0:T(8,128)(2,1)S(1)} %bitcast.424, bf16[768,768]{1,0:T(8,128)(2,1)S(1)} %copy-done.56), kind=kOutput, calls=%fused_computation.318 | convolution fusion | flops 4831838208 | bytes 20054016 | tf_op jit(solution)/shard_map/dot_general | solution.py:321
  438.8 16.7 %fusion.21 = (f32[768]{0:T(1024)S(1)}, f32[4096]{0:T(1024)S(1)}, f32[4096,768]{1,0:T(8,128)}) fusion(f32[2,4,512,768]{3,2,1,0:T(8,128)} %copy-done.4, f32[4096]{0:T(1024)S(1)} %bitcast.418, f32[768]{0:T(1024)S(1)} %copy-done.40, f32[4096,768]{1,0:T(8,128)} %fusion.158, bf16[4096,768]{1,0:T(8,128)(2,1)} %bitcast.386, bf16[768,768]{1,0:T(8,128)(2,1)S(1)} %copy-done.34), kind=kOutput, calls=%fused_computation.34 | convolution fusion | flops 4853853184 | bytes 45258752 | tf_op jit(solution)/shard_map/dot_general | solution.py:321
  455.5 3.6 fusion.26
  459.1 14.2 %fusion.18 = f32[4096,768]{1,0:T(8,128)} fusion(f32[2,4,512,768]{3,2,1,0:T(8,128)} %copy-done.4, f32[4096,768]{1,0:T(8,128)} %get-tuple-element.177, f32[4096]{0:T(1024)S(1)} %broadcast_multiply_fusion, f32[4096]{0:T(1024)S(1)} %copy-done.43, f32[768]{0:T(1024)S(1)} %copy-done.40, f32[4096]{0:T(1024)S(1)} %bitcast.419), kind=kLoop, calls=%fused_computation.31 | loop fusion | flops 15728640 | bytes 37800960 | tf_op jit(solution)/shard_map/sub | solution.py:504
  481.9 10.2 %copy_bitcast_fusion = f32[4,2,512,768]{3,2,1,0:T(8,128)} fusion(f32[2,4,512,768]{3,2,1,0:T(8,128)} %bitcast.376), kind=kLoop, calls=%fused_computation.35 | loop fusion | bytes 25165824 | tf_op jit(solution)/shard_map/transpose | solution.py:514
  492.1 7.2 fusion.162
  499.3 7.5 fusion.34
  510.3 77.5 %all-reduce = (f32[768]{0:T(1024)S(1)}, f32[12,12]{0,1:T(8,128)S(1)}, f32[12,12]{1,0:T(8,128)}, f32[768]{0:T(1024)S(1)}) all-reduce(f32[768]{0:T(1024)S(1)} %add.515, f32[12,12]{0,1:T(8,128)S(1)} %bitcast.420, f32[12,12]{1,0:T(8,128)S(1)} %reshape.546, f32[768]{0:T(1024)S(1)} %copy-done.47), channel_id=1, replica_groups=mesh['dp'=8,'blk'=4] {'dp','blk'}, use_global_device_ids=true, to_apply=%region_10.11 | all-reduce | flops 1824 | bytes 14592 | tf_op jit(solution)/shard_map/psum | solution.py:517
  589.6 3.2 slice.193
  599.6 2.9 collective-permute-start.36
  606.5 3.9 collective-permute-done.36
  612.4 4.3 collective-permute-done.9
  618.8 4.2 collective-permute-done.27
  624.7 4.3 collective-permute-done.18
  629.0 3.3 collective-permute-start.43
  635.7 2.5 collective-permute-done.42
  648.0 2.2 collective-permute-start.16
  654.1 2.8 bitcast_add_fusion.1
  657.4 3.2 collective-permute-start.13
  660.6 3.6 bitcast_add_fusion
  672.0 3.6 collective-permute-start.31
  683.1 3.7 collective-permute-start.25
  690.2 14.3 %collective-permute-done.54 = bf16[8,1,96,768]{3,2,1,0:T(8,128)(2,1)S(1)} collective-permute-done((bf16[8,1,96,768]{3,2,1,0:T(8,128)(2,1)S(1)}, bf16[8,1,96,768]{3,2,1,0:T(8,128)(2,1)S(1)}, u32[]{:S(2)}, u32[]{:S(2)}) %collective-permute-start.54) | collective-permute-done | bytes 1179680 | tf_op jit(solution)/shard_map/ppermute | solution.py:325
  705.1 2.9 collective-permute-start.22
  713.3 16.5 %collective-permute-done.45 = bf16[8,1,24,3072]{3,2,1,0:T(8,128)(2,1)S(1)} collective-permute-done((bf16[8,1,24,3072]{3,2,1,0:T(8,128)(2,1)S(1)}, bf16[8,1,24,3072]{3,2,1,0:T(8,128)(2,1)S(1)}, u32[]{:S(2)}, u32[]{:S(2)}) %collective-permute-start.45) | collective-permute-done | bytes 1179680 | tf_op jit(solution)/shard_map/ppermute | solution.py:325
  734.3 3.6 collective-permute-start.58
  739.3 10.8 %collective-permute-start.57 = (bf16[96,768]{1,0:T(8,128)(2,1)S(1)}, bf16[96,768]{1,0:T(8,128)(2,1)S(1)}, u32[]{:S(2)}, u32[]{:S(2)}) collective-permute-start(bf16[96,768]{1,0:T(8,128)(2,1)S(1)} %get-tuple-element.119), channel_id=1, source_target_pairs={{0,12},{4,8},{8,4},{12,0},{16,28},{20,24},{24,20},{28,16},{1,13},{... | collective-permute-start | bytes 442376 | tf_op jit(solution)/shard_map/ppermute | solution.py:325
  752.5 2.6 collective-permute-done.59
  761.4 4.8 collective-permute-start.49
  766.2 2.3 collective-permute-start.47
  769.4 2.4 collective-permute-done.50
  775.7 3.3 fusion.35
  (339 shorter events, 127.0 us)
Async XLA Ops:
  0.7 37.6 %collective-permute-start = (bf16[1,2,512,768]{3,2,1,0:T(8,128)(2,1)}, bf16[1,2,512,768]{3,2,1,0:T(8,128)(2,1)S(1)}, u32[]{:S(2)}, u32[]{:S(2)}) collective-permute-start(bf16[1,2,512,768]{3,2,1,0:T(8,128)(2,1)} %bitcast.393), channel_id=1, source_target_pairs={{0,2},{1,3},{2,0},{3,1},{4,6},{5,7},{6,4},{7,5},{8,10},{9,11},{10,... | collective-permute-start | bytes 4718600 | tf_op jit(solution)/shard_map/ppermute | solution.py:325
  41.7 29.2 %collective-permute-start.1 = (bf16[2,2,512,768]{3,2,1,0:T(8,128)(2,1)}, bf16[2,2,512,768]{3,2,1,0:T(8,128)(2,1)}, u32[]{:S(2)}, u32[]{:S(2)}) collective-permute-start(bf16[2,2,512,768]{3,2,1,0:T(8,128)(2,1)} %pad_maximum_fusion), channel_id=1, source_target_pairs={{0,1},{1,0},{2,3},{3,2},{4,5},{5,4},{6,7},{7,6},{8,9},{9,8},{10,11... | collective-permute-start | bytes 9437192 | tf_op jit(solution)/shard_map/ppermute | solution.py:325
  43.3 23.8 %collective-permute-start.4 = (bf16[2,256,768]{2,1,0:T(8,128)(2,1)}, bf16[2,256,768]{2,1,0:T(8,128)(2,1)}, u32[]{:S(2)}, u32[]{:S(2)}) collective-permute-start(bf16[2,256,768]{2,1,0:T(8,128)(2,1)} %gather_fusion.4), channel_id=1, source_target_pairs={{0,0},{1,2},{2,3},{3,1},{4,4},{5,6},{6,7},{7,5},{8,8},{9,10},{10,1... | collective-permute-start | bytes 2359304 | tf_op jit(solution)/shard_map/ppermute | solution.py:410
  52.2 16.2 %collective-permute-start.5 = (bf16[2,256,768]{2,1,0:T(8,128)(2,1)}, bf16[2,256,768]{2,1,0:T(8,128)(2,1)}, u32[]{:S(2)}, u32[]{:S(2)}) collective-permute-start(bf16[2,256,768]{2,1,0:T(8,128)(2,1)} %gather_fusion.5), channel_id=1, source_target_pairs={{0,1},{1,3},{2,2},{3,0},{4,5},{5,7},{6,6},{7,4},{8,9},{9,11},{10,1... | collective-permute-start | bytes 2359304 | tf_op jit(solution)/shard_map/ppermute | solution.py:410
  106.3 59.8 %copy-start.14 = (bf16[256,768]{1,0:T(8,128)(2,1)}, bf16[256,768]{1,0:T(8,128)(2,1)S(1)}, u32[]{:S(2)}) copy-start(bf16[256,768]{1,0:T(8,128)(2,1)S(1)} %get-tuple-element.184) | copy-start | bytes 1179652
  249.7 349.9 %collective-permute-start.2 = (bf16[2,256,768]{2,1,0:T(8,128)(2,1)}, bf16[2,256,768]{2,1,0:T(8,128)(2,1)}, u32[]{:S(2)}, u32[]{:S(2)}) collective-permute-start(bf16[2,256,768]{2,1,0:T(8,128)(2,1)} %gather_fusion.2), channel_id=1, source_target_pairs={{0,0},{2,1},{3,2},{1,3},{4,4},{6,5},{7,6},{5,7},{8,8},{10,9},{11,1... | collective-permute-start | bytes 2359304 | tf_op jit(solution)/shard_map/ppermute | solution.py:410
  257.1 346.6 %collective-permute-start.3 = (bf16[2,256,768]{2,1,0:T(8,128)(2,1)}, bf16[2,256,768]{2,1,0:T(8,128)(2,1)}, u32[]{:S(2)}, u32[]{:S(2)}) collective-permute-start(bf16[2,256,768]{2,1,0:T(8,128)(2,1)} %gather_fusion.3), channel_id=1, source_target_pairs={{1,0},{3,1},{2,2},{0,3},{5,4},{7,5},{6,6},{4,7},{9,8},{11,9},{10,1... | collective-permute-start | bytes 2359304 | tf_op jit(solution)/shard_map/ppermute | solution.py:410
  287.4 305.5 %collective-permute-start.35 = (bf16[8,2,24,768]{3,2,1,0:T(8,128)(2,1)}, bf16[8,2,24,768]{3,2,1,0:T(8,128)(2,1)}, u32[]{:S(2)}, u32[]{:S(2)}) collective-permute-start(bf16[8,2,24,768]{3,2,1,0:T(8,128)(2,1)} %fusion.51), channel_id=1, source_target_pairs={{0,1},{1,0},{2,3},{3,2},{4,5},{5,4},{6,7},{7,6},{8,9},{9,8},{10,11... | collective-permute-start | bytes 1769480 | tf_op jit(solution)/shard_map/ppermute | solution.py:325
  288.0 111.0 %copy-start.25 = (bf16[768,1024]{1,0:T(8,128)(2,1)S(1)}, bf16[768,1024]{1,0:T(8,128)(2,1)}, u32[]{:S(2)}) copy-start(bf16[768,1024]{1,0:T(8,128)(2,1)} %copy.111) | copy-start | bytes 4718596
  402.9 192.9 %collective-permute-start.8 = (bf16[8,2,24,768]{3,2,1,0:T(8,128)(2,1)}, bf16[8,2,24,768]{3,2,1,0:T(8,128)(2,1)}, u32[]{:S(2)}, u32[]{:S(2)}) collective-permute-start(bf16[8,2,24,768]{3,2,1,0:T(8,128)(2,1)} %fusion.48), channel_id=1, source_target_pairs={{0,1},{1,0},{2,3},{3,2},{4,5},{5,4},{6,7},{7,6},{8,9},{9,8},{10,11... | collective-permute-start | bytes 1769480 | tf_op jit(solution)/shard_map/ppermute | solution.py:325
  424.1 173.1 %collective-permute-start.26 = (bf16[8,2,24,768]{3,2,1,0:T(8,128)(2,1)}, bf16[8,2,24,768]{3,2,1,0:T(8,128)(2,1)}, u32[]{:S(2)}, u32[]{:S(2)}) collective-permute-start(bf16[8,2,24,768]{3,2,1,0:T(8,128)(2,1)} %fusion.50), channel_id=1, source_target_pairs={{0,1},{1,0},{2,3},{3,2},{4,5},{5,4},{6,7},{7,6},{8,9},{9,8},{10,11... | collective-permute-start | bytes 1769480 | tf_op jit(solution)/shard_map/ppermute | solution.py:325
  593.1 64.4 %collective-permute-start.53 = (bf16[8,2,96,768]{3,2,1,0:T(8,128)(2,1)S(1)}, bf16[8,2,96,768]{3,2,1,0:T(8,128)(2,1)}, u32[]{:S(2)}, u32[]{:S(2)}) collective-permute-start(bf16[8,2,96,768]{3,2,1,0:T(8,128)(2,1)S(1)} %copy-done.22), channel_id=1, source_target_pairs={{0,1},{1,0},{2,3},{3,2},{4,5},{5,4},{6,7},{7,6},{8,9},{9,8},{10,11... | collective-permute-start | bytes 7077896 | tf_op jit(solution)/shard_map/ppermute | solution.py:325
  595.8 3.4 collective-permute-start.17
  597.2 53.6 %collective-permute-start.44 = (bf16[8,2,24,3072]{3,2,1,0:T(8,128)(2,1)S(1)}, bf16[8,2,24,3072]{3,2,1,0:T(8,128)(2,1)S(1)}, u32[]{:S(2)}, u32[]{:S(2)}) collective-permute-start(bf16[8,2,24,3072]{3,2,1,0:T(8,128)(2,1)S(1)} %copy-done.23), channel_id=1, source_target_pairs={{0,1},{1,0},{2,3},{3,2},{4,5},{5,4},{6,7},{7,6},{8,9},{9,8},{10,11... | collective-permute-start | bytes 7077896 | tf_op jit(solution)/shard_map/ppermute | solution.py:325
  599.2 88.4 %collective-permute-start.6 = (bf16[2,2,512,768]{3,2,1,0:T(8,128)(2,1)S(1)}, bf16[2,2,512,768]{3,2,1,0:T(8,128)(2,1)}, u32[]{:S(2)}, u32[]{:S(2)}) collective-permute-start(bf16[2,2,512,768]{3,2,1,0:T(8,128)(2,1)S(1)} %slice.193), channel_id=1, source_target_pairs={{0,1},{1,0},{2,3},{3,2},{4,5},{5,4},{6,7},{7,6},{8,9},{9,8},{10,11... | collective-permute-start | bytes 9437192 | tf_op jit(solution)/shard_map/ppermute | solution.py:325
  599.6 10.8 %collective-permute-start.36 = (bf16[8,1,24,768]{3,2,1,0:T(8,128)(2,1)S(1)}, bf16[8,1,24,768]{3,2,1,0:T(8,128)(2,1)S(1)}, u32[]{:S(2)}, u32[]{:S(2)}) collective-permute-start(bf16[8,1,24,768]{3,2,1,0:T(8,128)(2,1)S(1)} %dynamic-slice_convert_fusion.7), channel_id=1, source_target_pairs={{0,2},{1,3},{2,0},{3,1},{4,6},{5,7},{6,4},{7,5},{8,10},{9,11},{10,... | collective-permute-start | bytes 884744 | tf_op jit(solution)/shard_map/ppermute | solution.py:325
  603.7 13.0 %collective-permute-start.9 = (bf16[8,1,24,768]{3,2,1,0:T(8,128)(2,1)S(1)}, bf16[8,1,24,768]{3,2,1,0:T(8,128)(2,1)S(1)}, u32[]{:S(2)}, u32[]{:S(2)}) collective-permute-start(bf16[8,1,24,768]{3,2,1,0:T(8,128)(2,1)S(1)} %dynamic-slice_convert_fusion.10), channel_id=1, source_target_pairs={{0,2},{1,3},{2,0},{3,1},{4,6},{5,7},{6,4},{7,5},{8,10},{9,11},{10,... | collective-permute-start | bytes 884744 | tf_op jit(solution)/shard_map/ppermute | solution.py:325
  610.4 12.6 %collective-permute-start.27 = (bf16[8,1,24,768]{3,2,1,0:T(8,128)(2,1)S(1)}, bf16[8,1,24,768]{3,2,1,0:T(8,128)(2,1)S(1)}, u32[]{:S(2)}, u32[]{:S(2)}) collective-permute-start(bf16[8,1,24,768]{3,2,1,0:T(8,128)(2,1)S(1)} %dynamic-slice_convert_fusion.8), channel_id=1, source_target_pairs={{0,2},{1,3},{2,0},{3,1},{4,6},{5,7},{6,4},{7,5},{8,10},{9,11},{10,... | collective-permute-start | bytes 884744 | tf_op jit(solution)/shard_map/ppermute | solution.py:325
  616.7 12.3 %collective-permute-start.18 = (bf16[8,1,24,768]{3,2,1,0:T(8,128)(2,1)S(1)}, bf16[8,1,24,768]{3,2,1,0:T(8,128)(2,1)S(1)}, u32[]{:S(2)}, u32[]{:S(2)}) collective-permute-start(bf16[8,1,24,768]{3,2,1,0:T(8,128)(2,1)S(1)} %dynamic-slice_convert_fusion.9), channel_id=1, source_target_pairs={{0,2},{1,3},{2,0},{3,1},{4,6},{5,7},{6,4},{7,5},{8,10},{9,11},{10,... | collective-permute-start | bytes 884744 | tf_op jit(solution)/shard_map/ppermute | solution.py:325
  623.0 9.3 %collective-permute-start.37 = (bf16[24,768]{1,0:T(8,128)(2,1)S(1)}, bf16[24,768]{1,0:T(8,128)(2,1)S(1)}, u32[]{:S(2)}, u32[]{:S(2)}) collective-permute-start(bf16[24,768]{1,0:T(8,128)(2,1)S(1)} %get-tuple-element.136), channel_id=1, source_target_pairs={{0,4},{4,0},{8,12},{12,8},{16,20},{20,16},{24,28},{28,24},{1,5},{5... | collective-permute-start | bytes 110600 | tf_op jit(solution)/shard_map/ppermute | solution.py:325
  629.0 6.7 collective-permute-start.43
  632.4 5.8 collective-permute-start.42
  635.7 6.2 collective-permute-start.41
  638.2 5.0 collective-permute-start.40
  641.9 4.9 collective-permute-start.39
  643.2 4.8 collective-permute-start.38
  646.7 10.2 %collective-permute-start.10 = (bf16[24,768]{1,0:T(8,128)(2,1)S(1)}, bf16[24,768]{1,0:T(8,128)(2,1)S(1)}, u32[]{:S(2)}, u32[]{:S(2)}) collective-permute-start(bf16[24,768]{1,0:T(8,128)(2,1)S(1)} %get-tuple-element.157), channel_id=1, source_target_pairs={{0,4},{4,0},{8,12},{12,8},{16,20},{20,16},{24,28},{28,24},{1,5},{5... | collective-permute-start | bytes 110600 | tf_op jit(solution)/shard_map/ppermute | solution.py:325
  648.0 16.2 %collective-permute-start.16 = (bf16[24,768]{1,0:T(8,128)(2,1)S(1)}, bf16[24,768]{1,0:T(8,128)(2,1)S(1)}, u32[]{:S(2)}, u32[]{:S(2)}) collective-permute-start(bf16[24,768]{1,0:T(8,128)(2,1)S(1)} %get-tuple-element.158), channel_id=1, source_target_pairs={{0,28},{4,24},{8,20},{12,16},{16,12},{20,8},{24,4},{28,0},{1,29},{... | collective-permute-start | bytes 110600 | tf_op jit(solution)/shard_map/ppermute | solution.py:325
  652.3 12.2 %collective-permute-start.15 = (bf16[24,768]{1,0:T(8,128)(2,1)S(1)}, bf16[24,768]{1,0:T(8,128)(2,1)S(1)}, u32[]{:S(2)}, u32[]{:S(2)}) collective-permute-start(bf16[24,768]{1,0:T(8,128)(2,1)S(1)} %get-tuple-element.159), channel_id=1, source_target_pairs={{0,24},{4,28},{8,16},{12,20},{16,8},{20,12},{24,0},{28,4},{1,25},{... | collective-permute-start | bytes 110600 | tf_op jit(solution)/shard_map/ppermute | solution.py:325
  656.9 9.6 %collective-permute-start.14 = (bf16[24,768]{1,0:T(8,128)(2,1)S(1)}, bf16[24,768]{1,0:T(8,128)(2,1)S(1)}, u32[]{:S(2)}, u32[]{:S(2)}) collective-permute-start(bf16[24,768]{1,0:T(8,128)(2,1)S(1)} %get-tuple-element.160), channel_id=1, source_target_pairs={{0,20},{4,16},{8,28},{12,24},{16,4},{20,0},{24,12},{28,8},{1,21},{... | collective-permute-start | bytes 110600 | tf_op jit(solution)/shard_map/ppermute | solution.py:325
  657.4 10.3 %collective-permute-start.13 = (bf16[24,768]{1,0:T(8,128)(2,1)S(1)}, bf16[24,768]{1,0:T(8,128)(2,1)S(1)}, u32[]{:S(2)}, u32[]{:S(2)}) collective-permute-start(bf16[24,768]{1,0:T(8,128)(2,1)S(1)} %get-tuple-element.161), channel_id=1, source_target_pairs={{0,16},{4,20},{8,24},{12,28},{16,0},{20,4},{24,8},{28,12},{1,17},{... | collective-permute-start | bytes 110600 | tf_op jit(solution)/shard_map/ppermute | solution.py:325
  664.2 5.9 collective-permute-start.12
  664.5 7.5 collective-permute-start.11
  666.5 5.5 collective-permute-start.28
  667.8 7.9 %collective-permute-start.34 = (bf16[24,768]{1,0:T(8,128)(2,1)S(1)}, bf16[24,768]{1,0:T(8,128)(2,1)S(1)}, u32[]{:S(2)}, u32[]{:S(2)}) collective-permute-start(bf16[24,768]{1,0:T(8,128)(2,1)S(1)} %get-tuple-element.144), channel_id=1, source_target_pairs={{0,28},{4,24},{8,20},{12,16},{16,12},{20,8},{24,4},{28,0},{1,29},{... | collective-permute-start | bytes 110600 | tf_op jit(solution)/shard_map/ppermute | solution.py:325
  670.1 7.3 collective-permute-start.33
  672.0 5.9 collective-permute-start.32
  672.0 7.7 collective-permute-start.31
  675.6 28.9 %collective-permute-start.54 = (bf16[8,1,96,768]{3,2,1,0:T(8,128)(2,1)S(1)}, bf16[8,1,96,768]{3,2,1,0:T(8,128)(2,1)S(1)}, u32[]{:S(2)}, u32[]{:S(2)}) collective-permute-start(bf16[8,1,96,768]{3,2,1,0:T(8,128)(2,1)S(1)} %dynamic-slice_convert_fusion.1), channel_id=1, source_target_pairs={{0,2},{1,3},{2,0},{3,1},{4,6},{5,7},{6,4},{7,5},{8,10},{9,11},{10,... | collective-permute-start | bytes 3538952 | tf_op jit(solution)/shard_map/ppermute | solution.py:325
  677.4 4.9 collective-permute-start.30
  677.9 5.3 collective-permute-start.29
  679.7 50.1 %collective-permute-start.45 = (bf16[8,1,24,3072]{3,2,1,0:T(8,128)(2,1)S(1)}, bf16[8,1,24,3072]{3,2,1,0:T(8,128)(2,1)S(1)}, u32[]{:S(2)}, u32[]{:S(2)}) collective-permute-start(bf16[8,1,24,3072]{3,2,1,0:T(8,128)(2,1)S(1)} %dynamic-slice_convert_fusion.2), channel_id=1, source_target_pairs={{0,2},{1,3},{2,0},{3,1},{4,6},{5,7},{6,4},{7,5},{8,10},{9,11},{10,... | collective-permute-start | bytes 3538952 | tf_op jit(solution)/shard_map/ppermute | solution.py:325
  682.3 22.7 %collective-permute-start.19 = (bf16[24,768]{1,0:T(8,128)(2,1)S(1)}, bf16[24,768]{1,0:T(8,128)(2,1)S(1)}, u32[]{:S(2)}, u32[]{:S(2)}) collective-permute-start(bf16[24,768]{1,0:T(8,128)(2,1)S(1)} %get-tuple-element.150), channel_id=1, source_target_pairs={{0,4},{4,0},{8,12},{12,8},{16,20},{20,16},{24,28},{28,24},{1,5},{5... | collective-permute-start | bytes 110600 | tf_op jit(solution)/shard_map/ppermute | solution.py:325
  683.1 25.0 %collective-permute-start.25 = (bf16[24,768]{1,0:T(8,128)(2,1)S(1)}, bf16[24,768]{1,0:T(8,128)(2,1)S(1)}, u32[]{:S(2)}, u32[]{:S(2)}) collective-permute-start(bf16[24,768]{1,0:T(8,128)(2,1)S(1)} %get-tuple-element.151), channel_id=1, source_target_pairs={{0,28},{4,24},{8,20},{12,16},{16,12},{20,8},{24,4},{28,0},{1,29},{... | collective-permute-start | bytes 110600 | tf_op jit(solution)/shard_map/ppermute | solution.py:325
  687.5 21.4 %collective-permute-start.24 = (bf16[24,768]{1,0:T(8,128)(2,1)S(1)}, bf16[24,768]{1,0:T(8,128)(2,1)S(1)}, u32[]{:S(2)}, u32[]{:S(2)}) collective-permute-start(bf16[24,768]{1,0:T(8,128)(2,1)S(1)} %get-tuple-element.152), channel_id=1, source_target_pairs={{0,24},{4,28},{8,16},{12,20},{16,8},{20,12},{24,0},{28,4},{1,25},{... | collective-permute-start | bytes 110600 | tf_op jit(solution)/shard_map/ppermute | solution.py:325
  704.5 6.4 collective-permute-start.23
  705.1 7.5 collective-permute-start.22
  708.1 24.3 %collective-permute-start.21 = (bf16[24,768]{1,0:T(8,128)(2,1)S(1)}, bf16[24,768]{1,0:T(8,128)(2,1)S(1)}, u32[]{:S(2)}, u32[]{:S(2)}) collective-permute-start(bf16[24,768]{1,0:T(8,128)(2,1)S(1)} %get-tuple-element.155), channel_id=1, source_target_pairs={{0,12},{4,8},{8,4},{12,0},{16,28},{20,24},{24,20},{28,16},{1,13},{... | collective-permute-start | bytes 110600 | tf_op jit(solution)/shard_map/ppermute | solution.py:325
  708.9 25.4 %collective-permute-start.20 = (bf16[24,768]{1,0:T(8,128)(2,1)S(1)}, bf16[24,768]{1,0:T(8,128)(2,1)S(1)}, u32[]{:S(2)}, u32[]{:S(2)}) collective-permute-start(bf16[24,768]{1,0:T(8,128)(2,1)S(1)} %get-tuple-element.156), channel_id=1, source_target_pairs={{0,8},{4,12},{8,0},{12,4},{16,24},{20,28},{24,16},{28,20},{1,9},{5... | collective-permute-start | bytes 110600 | tf_op jit(solution)/shard_map/ppermute | solution.py:325
  710.9 64.8 %collective-permute-start.7 = (bf16[1,2,512,768]{3,2,1,0:T(8,128)(2,1)S(1)}, bf16[1,2,512,768]{3,2,1,0:T(8,128)(2,1)S(1)}, u32[]{:S(2)}, u32[]{:S(2)}) collective-permute-start(bf16[1,2,512,768]{3,2,1,0:T(8,128)(2,1)S(1)} %fusion.30), channel_id=1, source_target_pairs={{0,2},{1,3},{2,0},{3,1},{4,6},{5,7},{6,4},{7,5},{8,10},{9,11},{10,... | collective-permute-start | bytes 4718600 | tf_op jit(solution)/shard_map/ppermute | solution.py:325
  712.5 21.8 %collective-permute-start.55 = (bf16[96,768]{1,0:T(8,128)(2,1)S(1)}, bf16[96,768]{1,0:T(8,128)(2,1)S(1)}, u32[]{:S(2)}, u32[]{:S(2)}) collective-permute-start(bf16[96,768]{1,0:T(8,128)(2,1)S(1)} %get-tuple-element.114), channel_id=1, source_target_pairs={{0,4},{4,0},{8,12},{12,8},{16,20},{20,16},{24,28},{28,24},{1,5},{5... | collective-permute-start | bytes 442376 | tf_op jit(solution)/shard_map/ppermute | solution.py:325
  729.8 9.5 %collective-permute-start.61 = (bf16[96,768]{1,0:T(8,128)(2,1)S(1)}, bf16[96,768]{1,0:T(8,128)(2,1)S(1)}, u32[]{:S(2)}, u32[]{:S(2)}) collective-permute-start(bf16[96,768]{1,0:T(8,128)(2,1)S(1)} %get-tuple-element.115), channel_id=1, source_target_pairs={{0,28},{4,24},{8,20},{12,16},{16,12},{20,8},{24,4},{28,0},{1,29},{... | collective-permute-start | bytes 442376 | tf_op jit(solution)/shard_map/ppermute | solution.py:325
  732.4 17.9 %collective-permute-start.60 = (bf16[96,768]{1,0:T(8,128)(2,1)S(1)}, bf16[96,768]{1,0:T(8,128)(2,1)S(1)}, u32[]{:S(2)}, u32[]{:S(2)}) collective-permute-start(bf16[96,768]{1,0:T(8,128)(2,1)S(1)} %get-tuple-element.116), channel_id=1, source_target_pairs={{0,24},{4,28},{8,16},{12,20},{16,8},{20,12},{24,0},{28,4},{1,25},{... | collective-permute-start | bytes 442376 | tf_op jit(solution)/shard_map/ppermute | solution.py:325
  734.3 20.8 %collective-permute-start.59 = (bf16[96,768]{1,0:T(8,128)(2,1)S(1)}, bf16[96,768]{1,0:T(8,128)(2,1)S(1)}, u32[]{:S(2)}, u32[]{:S(2)}) collective-permute-start(bf16[96,768]{1,0:T(8,128)(2,1)S(1)} %get-tuple-element.117), channel_id=1, source_target_pairs={{0,20},{4,16},{8,28},{12,24},{16,4},{20,0},{24,12},{28,8},{1,21},{... | collective-permute-start | bytes 442376 | tf_op jit(solution)/shard_map/ppermute | solution.py:325
  734.3 22.5 %collective-permute-start.58 = (bf16[96,768]{1,0:T(8,128)(2,1)S(1)}, bf16[96,768]{1,0:T(8,128)(2,1)S(1)}, u32[]{:S(2)}, u32[]{:S(2)}) collective-permute-start(bf16[96,768]{1,0:T(8,128)(2,1)S(1)} %get-tuple-element.118), channel_id=1, source_target_pairs={{0,16},{4,20},{8,24},{12,28},{16,0},{20,4},{24,8},{28,12},{1,17},{... | collective-permute-start | bytes 442376 | tf_op jit(solution)/shard_map/ppermute | solution.py:325
  739.3 19.5 %collective-permute-start.57 = (bf16[96,768]{1,0:T(8,128)(2,1)S(1)}, bf16[96,768]{1,0:T(8,128)(2,1)S(1)}, u32[]{:S(2)}, u32[]{:S(2)}) collective-permute-start(bf16[96,768]{1,0:T(8,128)(2,1)S(1)} %get-tuple-element.119), channel_id=1, source_target_pairs={{0,12},{4,8},{8,4},{12,0},{16,28},{20,24},{24,20},{28,16},{1,13},{... | collective-permute-start | bytes 442376 | tf_op jit(solution)/shard_map/ppermute | solution.py:325
  750.3 11.0 %collective-permute-start.56 = (bf16[96,768]{1,0:T(8,128)(2,1)S(1)}, bf16[96,768]{1,0:T(8,128)(2,1)S(1)}, u32[]{:S(2)}, u32[]{:S(2)}) collective-permute-start(bf16[96,768]{1,0:T(8,128)(2,1)S(1)} %get-tuple-element.120), channel_id=1, source_target_pairs={{0,8},{4,12},{8,0},{12,4},{16,24},{20,28},{24,16},{28,20},{1,9},{5... | collective-permute-start | bytes 442376 | tf_op jit(solution)/shard_map/ppermute | solution.py:325
  755.1 6.3 collective-permute-start.46
  756.8 9.4 %collective-permute-start.52 = (bf16[24,3072]{1,0:T(8,128)(2,1)S(1)}, bf16[24,3072]{1,0:T(8,128)(2,1)S(1)}, u32[]{:S(2)}, u32[]{:S(2)}) collective-permute-start(bf16[24,3072]{1,0:T(8,128)(2,1)S(1)} %get-tuple-element.122), channel_id=1, source_target_pairs={{0,28},{4,24},{8,20},{12,16},{16,12},{20,8},{24,4},{28,0},{1,29},{... | collective-permute-start | bytes 442376 | tf_op jit(solution)/shard_map/ppermute | solution.py:325
  758.9 7.3 collective-permute-start.51
  761.4 10.4 %collective-permute-start.50 = (bf16[24,3072]{1,0:T(8,128)(2,1)S(1)}, bf16[24,3072]{1,0:T(8,128)(2,1)S(1)}, u32[]{:S(2)}, u32[]{:S(2)}) collective-permute-start(bf16[24,3072]{1,0:T(8,128)(2,1)S(1)} %get-tuple-element.124), channel_id=1, source_target_pairs={{0,20},{4,16},{8,28},{12,24},{16,4},{20,0},{24,12},{28,8},{1,21},{... | collective-permute-start | bytes 442376 | tf_op jit(solution)/shard_map/ppermute | solution.py:325
  761.4 11.4 %collective-permute-start.49 = (bf16[24,3072]{1,0:T(8,128)(2,1)S(1)}, bf16[24,3072]{1,0:T(8,128)(2,1)S(1)}, u32[]{:S(2)}, u32[]{:S(2)}) collective-permute-start(bf16[24,3072]{1,0:T(8,128)(2,1)S(1)} %get-tuple-element.125), channel_id=1, source_target_pairs={{0,16},{4,20},{8,24},{12,28},{16,0},{20,4},{24,8},{28,12},{1,17},{... | collective-permute-start | bytes 442376 | tf_op jit(solution)/shard_map/ppermute | solution.py:325
  766.2 8.7 %collective-permute-start.48 = (bf16[24,3072]{1,0:T(8,128)(2,1)S(1)}, bf16[24,3072]{1,0:T(8,128)(2,1)S(1)}, u32[]{:S(2)}, u32[]{:S(2)}) collective-permute-start(bf16[24,3072]{1,0:T(8,128)(2,1)S(1)} %get-tuple-element.126), channel_id=1, source_target_pairs={{0,12},{4,8},{8,4},{12,0},{16,28},{20,24},{24,20},{28,16},{1,13},{... | collective-permute-start | bytes 442376 | tf_op jit(solution)/shard_map/ppermute | solution.py:325
  766.2 8.7 %collective-permute-start.47 = (bf16[24,3072]{1,0:T(8,128)(2,1)S(1)}, bf16[24,3072]{1,0:T(8,128)(2,1)S(1)}, u32[]{:S(2)}, u32[]{:S(2)}) collective-permute-start(bf16[24,3072]{1,0:T(8,128)(2,1)S(1)} %get-tuple-element.127), channel_id=1, source_target_pairs={{0,8},{4,12},{8,0},{12,4},{16,24},{20,28},{24,16},{28,20},{1,9},{5... | collective-permute-start | bytes 442376 | tf_op jit(solution)/shard_map/ppermute | solution.py:325
  (68 other events, 948.9 us)
